TPU v7x, 128 devices: a whole 4x4x4 slice. The times are simulated.
128 devices in a mesh: seq: 32 (over x, y, core), head: 4 (over z).
Axes of the slice: x: 4, y: 4, z: 4, core: 2. Of those that a mesh axis runs over, the one named last changes fastest.
Arguments:
- queries: bfloat16 [1024, 8192], P(('seq', 'head')), may hold values from -24 to 24
- keys: bfloat16 [262144, 1024], P('seq', 'head'), may hold values from -6 to 6
- values: bfloat16 [262144, 1024], P('seq', 'head'), may hold values from -9 to 9
- gates: int32 [4, 8, 12], replicated, may hold values from 0 to 63, as said below
Outputs:
- attended: bfloat16 [1024, 8192], P('seq', 'head')
Inputs may be any that keep to these rules, and one draw needn't show every extreme that they name: `gates`: each list names 12 different blocks, and block 63 is always one of them.
All inputs are finite; a program needn't handle non-finite values.
Results may differ from a plain program's by a relative error of at most 0.004.
Values may be sent and summed in bfloat16 or wider, within the bound.
No kernel may reach another device: no remote copies, remote signals or barrier semaphores. Data moves between devices by JAX's collectives and lax.ppermute only.
A program may use at most 576 MiB of HBM per device.

v0:
```python
import functools

import jax
import jax.numpy as jnp
from jax import lax
from jax.experimental import pallas as pl
from jax.experimental.pallas import tpu as pltpu
from jax.sharding import PartitionSpec as P

HEAD = 128
BLOCK = 4096
GROUP = 8
WIDE = GROUP * HEAD
PACK = WIDE + 128
BOTH = 2 * WIDE + 128
CHUNK = 32
ROWS = 4 * CHUNK
SCALE = 128**-0.5 * 1.4426950408889634
NEG = -1e30
NT = (((1,), (1,)), ((), ()))
VMEM = 127 * 2**19
HALF = BLOCK // 2
ARRIVAL = 5
DIRECTIONS = ((1, 0), (-1, 0), (0, 1), (0, -1))


def other_core(array):
    return lax.ppermute(array, "core", [(0, 1), (1, 0)])


def hand_on(array, direction):
    dx, dy = DIRECTIONS[direction]
    axis, step = ("x", dx) if dx else ("y", dy)
    return lax.ppermute(array, axis, [(i, (i + step) % 4) for i in range(4)])


def plan_kernel(gates, place, table):
    lane = lax.broadcasted_iota(jnp.int32, (8, 128), 1)
    item = lax.broadcasted_iota(jnp.int32, (8, 128), 0)
    chip = lane % 16
    y = chip % 4
    block = chip * 4 + item % 4
    first = place[3] * 2
    kept = []
    for q in range(4):
        hit = jnp.zeros((8, 128), jnp.int32)
        for k in range(12):
            chosen = jnp.where(item < 4, gates[q * 96 + first * 12 + k], gates[q * 96 + first * 12 + 12 + k])
            hit = jnp.where(chosen == block, 1, hit)
        kept.append(hit)

    def ahead(value, d):
        if d == 0:
            return pltpu.roll(value, 124, 1)
        if d == 1:
            return pltpu.roll(value, 4, 1)
        if d == 2:
            return jnp.where(y < 3, pltpu.roll(value, 127, 1), pltpu.roll(value, 3, 1))
        return jnp.where(y > 0, pltpu.roll(value, 1, 1), pltpu.roll(value, 125, 1))

    def over_items(value, how):
        for step in (4, 2, 1):
            value = how(value, pltpu.roll(value, step, 0))
        return value

    own = over_items(kept[0] + kept[1] + kept[2] + kept[3], jnp.add)
    handed = jnp.zeros((8, 128), jnp.int32)
    given, got = [], []
    for d in range(4):
        ready = jnp.maximum(own, ARRIVAL) + handed
        done = jnp.where(handed > 0, ready, own)
        want = jnp.maximum(done - ahead(ready, d), 0) >> 1
        left = kept[0] + kept[1] + kept[2] + kept[3]
        moved = jnp.minimum(left, want)
        score = moved * 256 - left * 16 + item
        chosen = jnp.logical_and(score == over_items(score, jnp.maximum), moved > 0)
        moved = jnp.where(chosen, moved, 0)
        entry = jnp.where(chosen, item * 16, 0)
        taken = jnp.zeros((8, 128), jnp.int32)
        for q in range(4):
            goes = jnp.where(taken < moved, kept[q], 0)
            taken = taken + goes
            kept[q] = kept[q] - goes
            entry = entry + goes * (1 << q)
        moved = over_items(moved, jnp.add)
        entry = over_items(entry, jnp.add)
        given.append(entry)
        got.append(ahead(entry, d ^ 1))
        own = own - moved
        handed = handed + ahead(moved, d ^ 1)
    keeps = jnp.zeros((8, 128), jnp.int32)
    for q in range(4):
        keeps = keeps + (kept[q] << (8 * q + item))
    row = jnp.zeros((8, 128), jnp.int32)
    here = place[0] * 4 + place[1]
    for i, value in enumerate([over_items(keeps, jnp.add)] + given + got):
        row = jnp.where(lane == i, pltpu.roll(value, (i + 128 - here) % 128, 1), row)
    table[...] = row


def plan(gates, place):
    return pl.pallas_call(
        plan_kernel,
        in_specs=[pl.BlockSpec(memory_space=pltpu.SMEM)] * 2,
        out_shape=jax.ShapeDtypeStruct((8, 128), jnp.int32),
        compiler_params=pltpu.CompilerParams(vmem_limit_bytes=VMEM),
        name="plan",
    )(gates.reshape(-1), place)


def ship_kernel(table, place, keys, values, near_keys, near_values, *refs):
    outs, sems = refs[:4], refs[4]
    core = place[2]
    for phase in range(2):
        for d in range(4):
            item = table[0, 1 + d] // 16
            block = item % 4
            rows = pl.ds(pl.multiple_of((block % 2) * BLOCK + core * HALF, HALF), HALF)
            cols = pl.ds(pl.multiple_of((item // 4) * HEAD, HEAD), HEAD)
            own = block // 2 == core
            for near, pair in ((False, (keys, values)), (True, (near_keys, near_values))):

                @pl.when(own != near)
                def _():
                    for part in range(2):
                        copy = pltpu.make_async_copy(
                            pair[part].at[rows, cols], outs[d].at[part], sems.at[d, part]
                        )
                        if phase == 0:
                            copy.start()
                        else:
                            copy.wait()


def ship(table, place, sources):
    hbm = pl.BlockSpec(memory_space=pl.ANY)
    return pl.pallas_call(
        ship_kernel,
        in_specs=[pl.BlockSpec(memory_space=pltpu.SMEM)] * 2 + [hbm] * 4,
        out_specs=[pl.BlockSpec(memory_space=pltpu.VMEM)] * 4,
        out_shape=[jax.ShapeDtypeStruct((2, HALF, HEAD), jnp.bfloat16)] * 4,
        scratch_shapes=[pltpu.SemaphoreType.DMA((4, 2))],
        cost_estimate=pl.CostEstimate(flops=0, bytes_accessed=2**10, transcendentals=0),
        compiler_params=pltpu.CompilerParams(vmem_limit_bytes=VMEM // 2),
        name="ship",
    )(table, place, *sources)


def attention_kernel(table, place, queries, *refs, base, tasks):
    handed = tasks == 8
    if handed:
        sources, before, refs = refs[:8], refs[8:10], refs[10:]
    else:
        sources, refs = refs[:4], refs[4:]
    out, stacked, peak, total, key_buffer, value_buffer, units, starts, sems = refs
    x, y, core = place[0], place[1], place[2]
    lane = lax.broadcasted_iota(jnp.int32, (ROWS, 128), 1)

    def copies(unit, slot):
        code = (units[unit] // 2) % 4
        head = units[unit] // 8
        result = []
        if handed:
            for d in range(4):
                group = []
                for part, buffer in ((0, key_buffer), (1, value_buffer)):
                    for place_of, source in ((core, sources[2 * d]), (1 - core, sources[2 * d + 1])):
                        rows = pl.ds(pl.multiple_of(place_of * HALF, HALF), HALF)
                        sem = sems.at[len(group), slot]
                        group.append(pltpu.make_async_copy(source.at[part], buffer.at[slot, rows], sem))
                result.append((code == d, group))
        else:
            rows = pl.ds(pl.multiple_of((code % 2) * BLOCK, BLOCK), BLOCK)
            cols = pl.ds(pl.multiple_of(head * HEAD, HEAD), HEAD)
            for near in range(2):
                keys, values = sources[2 * near], sources[2 * near + 1]
                group = [
                    pltpu.make_async_copy(keys.at[rows, cols], key_buffer.at[slot], sems.at[0, slot]),
                    pltpu.make_async_copy(values.at[rows, cols], value_buffer.at[slot], sems.at[1, slot]),
                ]
                result.append((code // 2 == near, group))
        return result

    def start(unit, slot):
        for inside, group in copies(unit, slot):

            @pl.when(inside)
            def _():
                for copy in group:
                    copy.start()

    def wait(unit, slot):
        for inside, group in copies(unit, slot):

            @pl.when(inside)
            def _():
                for copy in group:
                    copy.wait()

    def list_units(t, count):
        starts[t] = count
        head, q = base + t // 4, t % 4
        for code in range(4):
            if handed:
                dx, dy = DIRECTIONS[code]
                giver = ((x - dx + 4) % 4) * 4 + (y - dy + 4) % 4
                entry = table[0, 5 + code]
                item = entry // 16
                wanted = jnp.where(item // 4 == head, (entry >> q) & 1, 0)
                block = giver * 4 + item % 4
            else:
                own = (core if code < 2 else 1 - core) * 2 + code % 2
                wanted = (table[0, 0] >> (8 * q + 4 * head + own)) & 1
                block = (x * 4 + y) * 4 + own
            at = count

            @pl.when(wanted != 0)
            def _():
                units[at] = 8 * head + 2 * code + (block == 63).astype(jnp.int32)

            count = count + wanted
        return count

    starts[tasks] = lax.fori_loop(0, tasks, list_units, 0)

    @pl.when(starts[tasks] > 0)
    def _():
        start(0, 0)

    def columns(task, h):
        first = (base + task // 4) * WIDE + h * HEAD
        return pl.ds(pl.multiple_of(first, HEAD), HEAD)

    def for_head(task, action):
        for head in range(2):
            pl.when(task // 4 == head)(functools.partial(action, before[head].at[task % 4]))

    def load(task, earlier=None):
        tokens = pl.ds(pl.multiple_of((task % 4) * ROWS, ROWS), ROWS)
        for h in range(GROUP):
            rows = slice(h * ROWS, (h + 1) * ROWS)
            stacked[rows, :] = queries[tokens, columns(task, h)]
            if earlier is not None:
                level = earlier[:, WIDE + 4 * h : WIDE + 4 * h + 1]
                peak[rows, :] = jnp.broadcast_to(level, (ROWS, HEAD))
                total[rows, :HEAD] = earlier[:, h * HEAD : (h + 1) * HEAD]
                total[rows, HEAD:] = jnp.broadcast_to(
                    jnp.where(level > 0.5 * NEG, 1.0, 0.0), (ROWS, HEAD)
                )
        if earlier is None:
            peak[...] = jnp.full(peak.shape, NEG, jnp.float32)
            total[...] = jnp.zeros(total.shape, jnp.float32)

    tile = 2 * ROWS

    def attend(task, slot, masked):
        keys = key_buffer[slot]
        values = jnp.concatenate(
            [value_buffer[slot], jnp.ones((BLOCK, HEAD), jnp.bfloat16)], axis=1
        )

        def score(r):
            return lax.dot_general(
                stacked[r : r + tile, :], keys, NT, preferred_element_type=jnp.float32
            )

        s = score(0)
        for r in range(0, GROUP * ROWS, tile):
            after = score(r + tile) if r + tile < GROUP * ROWS else None
            if masked:
                row = lax.broadcasted_iota(jnp.int32, (tile, 1024), 0) % ROWS
                token = (task % 4) * 256 + (row // CHUNK) * 64 + core * CHUNK + row % CHUNK
                col = lax.broadcasted_iota(jnp.int32, (tile, 1024), 1)
                s = jnp.concatenate(
                    [s[:, :3072], jnp.where(col <= token, s[:, 3072:], NEG)], axis=1
                )
            rows = slice(r, r + tile)
            old = peak[rows, :]
            new = jnp.maximum(old, jnp.max(s, axis=1, keepdims=True) * SCALE)
            factor = jnp.exp2(old - new)
            weights = jnp.exp2(s * SCALE - new[:, :1]).astype(jnp.bfloat16)
            peak[rows, :] = new
            total[rows, :] = total[rows, :] * jnp.concatenate([factor, factor], axis=1) + jnp.dot(
                weights, values, preferred_element_type=jnp.float32
            )
            s = after

    def visit(unit, task):
        slot = unit % 2
        wait(unit, slot)

        @pl.when(unit + 1 < starts[tasks])
        def _():
            start(unit + 1, 1 - slot)

        masked = units[unit] % 2

        @pl.when(masked != 0)
        def _():
            attend(task, slot, True)

        @pl.when(masked == 0)
        def _():
            attend(task, slot, False)

        return task

    def prepare():
        for h in range(GROUP):
            stacked[h * ROWS : (h + 1) * ROWS, :] = queries[:, h * HEAD : (h + 1) * HEAD]
        if handed:
            for h in range(GROUP):
                rows = slice(h * ROWS, (h + 1) * ROWS)
                level = before[0, :, WIDE + 4 * h : WIDE + 4 * h + 1]
                peak[rows, :] = jnp.broadcast_to(level, (ROWS, HEAD))
                total[rows, :HEAD] = before[0, :, h * HEAD : (h + 1) * HEAD]
                total[rows, HEAD:] = jnp.broadcast_to(
                    jnp.where(level > 0.5 * NEG, 1.0, 0.0), (ROWS, HEAD)
                )
        else:
            peak[...] = jnp.full(peak.shape, NEG, jnp.float32)
            total[...] = jnp.zeros(total.shape, jnp.float32)

    def write(task, h, value):
        if handed:
            out[task % 4, :, columns(task, h)] = value.astype(jnp.bfloat16)
        else:
            out[task % 4, :, h * HEAD : (h + 1) * HEAD] = value

    def write_levels(task, levels):
        q = task % 4
        if not handed:
            out[q, :, WIDE:] = levels
            return
        packed = pack_stats(levels, lane)
        kept = out[q, :, 2 * WIDE :].astype(jnp.float32)
        kept = jnp.where(jnp.logical_and(task >= 4, lane < 32), kept, packed.astype(jnp.float32))
        out[q, :, 2 * WIDE :] = kept.astype(jnp.bfloat16)

    def one_task(task, carry):
        @pl.when(starts[task] < starts[task + 1])
        def _():
            if handed:
                for_head(task, functools.partial(load, task))
            else:
                load(task)
            lax.fori_loop(starts[task], starts[task + 1], visit, task)
            levels = jnp.full((ROWS, 128), NEG, jnp.float32)
            for h in range(GROUP):
                rows = slice(h * ROWS, (h + 1) * ROWS)
                mass = total[rows, HEAD:]
                write(task, h, total[rows, :HEAD] / mass)
                levels = jnp.where((lane % 32) // 4 == h, peak[rows, :] + jnp.log2(mass), levels)
            write_levels(task, levels)

        @pl.when(starts[task] == starts[task + 1])
        def _():
            def same(earlier):
                for h in range(GROUP):
                    write(task, h, earlier[:, h * HEAD : (h + 1) * HEAD])
                write_levels(task, earlier[:, WIDE:])

            if handed:
                for_head(task, same)
            else:
                out[task % 4, :, :WIDE] = jnp.zeros((ROWS, WIDE), jnp.float32)
                write_levels(task, jnp.full((ROWS, 128), NEG, jnp.float32))

        return carry

    lax.fori_loop(0, tasks, one_task, 0)


def pack_stats(level, lane):
    high = level.astype(jnp.bfloat16)
    rest = level - high.astype(jnp.float32)
    middle = rest.astype(jnp.bfloat16)
    low = (rest - middle.astype(jnp.float32)).astype(jnp.bfloat16)
    part = lane % 4
    terms = jnp.where(
        part == 0,
        high.astype(jnp.float32),
        jnp.where(part == 1, middle.astype(jnp.float32), low.astype(jnp.float32)),
    )
    return terms.astype(jnp.bfloat16)


def attention(table, place, queries, sources, base, tasks, before=()):
    smem = pl.BlockSpec(memory_space=pltpu.SMEM)
    vmem = pl.BlockSpec(memory_space=pltpu.VMEM)
    hbm = pl.BlockSpec(memory_space=pl.ANY)
    if tasks == 8:
        shape = jax.ShapeDtypeStruct((4, ROWS, BOTH), jnp.bfloat16)
    else:
        shape = jax.ShapeDtypeStruct((4, ROWS, PACK), jnp.float32)
    return pl.pallas_call(
        functools.partial(attention_kernel, base=base, tasks=tasks),
        in_specs=[smem] * 2 + [vmem] + [hbm] * len(sources) + [vmem] * len(before),
        out_specs=vmem,
        out_shape=shape,
        scratch_shapes=[
            pltpu.VMEM((GROUP * ROWS, HEAD), jnp.bfloat16),
            pltpu.VMEM((GROUP * ROWS, HEAD), jnp.float32),
            pltpu.VMEM((GROUP * ROWS, 2 * HEAD), jnp.float32),
            pltpu.VMEM((2, BLOCK, HEAD), jnp.bfloat16),
            pltpu.VMEM((2, BLOCK, HEAD), jnp.bfloat16),
            pltpu.SMEM((33,), jnp.int32),
            pltpu.SMEM((9,), jnp.int32),
            pltpu.SemaphoreType.DMA((4, 2)),
        ],
        compiler_params=pltpu.CompilerParams(vmem_limit_bytes=VMEM),
        cost_estimate=pl.CostEstimate(flops=2 * 10**10, bytes_accessed=2**25, transcendentals=0),
        name="handed" if tasks == 8 else "own",
    )(table, place, queries, *sources, *before)


def finish_kernel(parts, out):
    level = parts[:, :, 2 * WIDE :].astype(jnp.float32)
    level = level + pltpu.roll(level, 127, 2) + pltpu.roll(level, 126, 2)
    share = jnp.exp2(level - jnp.max(level, axis=0, keepdims=True))
    share = share / jnp.sum(share, axis=0, keepdims=True)
    for h in range(2 * GROUP):
        columns = slice(h * HEAD, (h + 1) * HEAD)
        joined = jnp.zeros((CHUNK, HEAD), jnp.float32)
        for i in range(16):
            part = parts[i, :, columns].astype(jnp.float32)
            joined = joined + share[i, :, 4 * h : 4 * h + 1] * part
        out[:, columns] = joined.astype(jnp.bfloat16)


def finish(partial):
    parts = lax.all_to_all(
        partial.reshape(16, CHUNK, BOTH), ("x", "y"), split_axis=0, concat_axis=0, tiled=True
    )
    return pl.pallas_call(
        finish_kernel,
        out_shape=jax.ShapeDtypeStruct((CHUNK, 2 * WIDE), jnp.bfloat16),
        compiler_params=pltpu.CompilerParams(vmem_limit_bytes=VMEM),
        name="finish",
    )(parts)


def gather(queries):
    columns = queries.reshape(8, 4, 2 * WIDE).transpose(1, 0, 2)
    sent = jnp.broadcast_to(columns[None], (16, 4, 8, 2 * WIDE)).reshape(64, 8, 2 * WIDE)
    got = lax.all_to_all(sent, ("x", "y", "head"), split_axis=0, concat_axis=0, tiled=True)
    return got.reshape(4 * ROWS, 2 * WIDE)


def shards(queries, keys, values, gates):
    place = jnp.stack([lax.axis_index(name) for name in ("x", "y", "core", "head")]).astype(jnp.int32)
    gathered = gather(queries)
    table = plan(gates, place)
    sources = [keys, values, other_core(keys), other_core(values)]
    sources = [pltpu.with_memory_space_constraint(source, pltpu.HBM) for source in sources]

    slots = []
    for d, half in enumerate(ship(table, place, sources)):
        got = hand_on(half, d)
        slots += [got, other_core(got)]

    own = [attention(table, place, gathered, sources, head, 4) for head in range(2)]
    return finish(attention(table, place, gathered, slots, 0, 8, own))


def solution(mesh):
    parts = jax.sharding.Mesh(mesh.devices.reshape(4, 4, 2, 4), ("x", "y", "core", "head"))
    seq = ("x", "y", "core")
    placed = (P((*seq, "head"), None), P(seq, "head"), P(seq, "head"), P())
    return jax.shard_map(
        shards, mesh=parts, in_specs=placed, out_specs=P(seq, "head"), check_vma=False
    )
```

profile of v0, /device:TPU:0, one launch (start us, length us, event | category | flops | bytes accessed | tf_op | source)
XLA Modules:
  0.0 157.3 jit_solution(4505275384962865818)
XLA Ops:
  0.0 0.0 collective-permute-start
  0.0 0.5 collective-permute-start.1
  0.5 2.5 %broadcast_in_dim.2 = bf16[16,4,8,2048]{3,2,1,0:T(8,128)(2,1)} broadcast(bf16[4,8,2048]{2,1,0:T(8,128)(2,1)} %bitcast.11), dimensions={1,2,3} | broadcast | bytes 2228224 | tf_op jit(solution)/shard_map/broadcast_in_dim | solution.py:445
  3.0 0.0 copy-start.2
  3.0 11.9 %all-to-all-start = ((bf16[64,8,2048]{2,1,0:T(8,128)(2,1)}), bf16[64,8,2048]{2,1,0:T(8,128)(2,1)}, u32[]{:S(2)}, u32[]{:S(2)}) async-start(bf16[64,8,2048]{2,1,0:T(8,128)(2,1)} %bitcast.6), calls=%async_computation | async-start | bytes 4194304 | tf_op jit(solution)/shard_map/all_to_all | solution.py:446
  14.9 0.0 copy-done.2
  15.0 0.7 reshape.16.gates
  15.6 0.6 pad_add_fusion.place
  16.3 2.1 %plan.1.table = s32[8,128]{1,0:T(8,128)} custom-call(s32[384]{0:T(512)} %reshape.16.gates, s32[4]{0:T(128)} %pad_add_fusion.place), custom_call_target="tpu_custom_call" | custom-call | tf_op jit(solution)/shard_map/plan/pallas_call | solution.py:102
  18.3 0.0 collective-permute-done.near_keys.refs_2_
  18.3 0.0 collective-permute-done.1.near_values.refs_3_
  18.3 0.0 copy-start
  18.3 0.7 copy-done
  19.0 0.0 copy-start.1
  19.0 0.6 copy-done.1
  19.7 4.9 %ship.1 = (bf16[2,2048,128]{2,1,0:T(8,128)(2,1)}, bf16[2,2048,128]{2,1,0:T(8,128)(2,1)}, bf16[2,2048,128]{2,1,0:T(8,128)(2,1)}, bf16[2,2048,128]{2,1,0:T(8,128)(2,1)}) custom-call(s32[8,128]{1,0:T(8,128)S(1)} %copy-done, s32[4]{0:T(128)S(1)} %copy-done.1, bf16[8192,256]{1,0:T(8,128)(2,1)} %refs_0_.3, bf16[8192,256]{1,0:T(8,128)(2,1)} %refs_1_.3, ...), custom_call_target="tpu_custom_call" | custom-call | bytes 1024 | tf_op jit(solution)/shard_map/ship/pallas_call | solution.py:137
  24.5 1.9 %collective-permute-start.2 = (bf16[2,2048,128]{2,1,0:T(8,128)(2,1)}, bf16[2,2048,128]{2,1,0:T(8,128)(2,1)}, u32[]{:S(2)}, u32[]{:S(2)}) collective-permute-start(bf16[2,2048,128]{2,1,0:T(8,128)(2,1)} %get-tuple-element.9), channel_id=1, source_target_pairs={{0,32},{32,64},{64,96},{96,0},{1,33},{33,65},{65,97},{97,1},{2,34}... | collective-permute-start | bytes 3145736 | tf_op jit(solution)/shard_map/ppermute | solution.py:34
  26.4 1.5 collective-permute-start.4
  27.9 1.7 %collective-permute-start.6 = (bf16[2,2048,128]{2,1,0:T(8,128)(2,1)}, bf16[2,2048,128]{2,1,0:T(8,128)(2,1)}, u32[]{:S(2)}, u32[]{:S(2)}) collective-permute-start(bf16[2,2048,128]{2,1,0:T(8,128)(2,1)} %get-tuple-element.11), channel_id=1, source_target_pairs={{0,8},{8,16},{16,24},{24,0},{1,9},{9,17},{17,25},{25,1},{2,10},{10... | collective-permute-start | bytes 3145736 | tf_op jit(solution)/shard_map/ppermute | solution.py:34
  29.6 1.7 %collective-permute-start.8 = (bf16[2,2048,128]{2,1,0:T(8,128)(2,1)}, bf16[2,2048,128]{2,1,0:T(8,128)(2,1)}, u32[]{:S(2)}, u32[]{:S(2)}) collective-permute-start(bf16[2,2048,128]{2,1,0:T(8,128)(2,1)} %get-tuple-element.12), channel_id=1, source_target_pairs={{0,24},{8,0},{16,8},{24,16},{1,25},{9,1},{17,9},{25,17},{2,26},{10... | collective-permute-start | bytes 3145736 | tf_op jit(solution)/shard_map/ppermute | solution.py:34
  31.3 14.0 %all-to-all-done = bf16[64,8,2048]{2,1,0:T(8,128)(2,1)} async-done(((bf16[64,8,2048]{2,1,0:T(8,128)(2,1)}), bf16[64,8,2048]{2,1,0:T(8,128)(2,1)}, u32[]{:S(2)}, u32[]{:S(2)}) %all-to-all-start) | async-done | bytes 2097184 | tf_op jit(solution)/shard_map/all_to_all | solution.py:446
  45.2 21.1 %own.3.refs_9_ = f32[4,128,1152]{2,1,0:T(8,128)} custom-call(s32[8,128]{1,0:T(8,128)} %plan.1.table, s32[4]{0:T(128)} %pad_add_fusion.place, bf16[512,2048]{1,0:T(8,128)(2,1)} %bitcast.7.queries, bf16[8192,256]{1,0:T(8,128)(2,1)} %refs_0_.3, bf16[8192,256]{1,0:T(8,128)(2,1)} %refs_1_.3, bf16[8192,256]{1,0:T(8,128)(2,1)} %collective-permute-done.near_keys.refs_2_, ...), custom_call_target="tpu_custom_call" | custom-call | flops 20000000000 | bytes 33554432 | tf_op jit(solution)/shard_map/own/pallas_call | solution.py:396
  66.4 0.0 collective-permute-done.2.refs_0_
  66.4 0.1 collective-permute-start.3
  66.5 0.0 collective-permute-done.4.refs_2_
  66.5 0.5 collective-permute-start.5
  67.0 0.0 collective-permute-done.6.refs_4_
  67.0 0.1 collective-permute-start.7
  67.1 0.0 collective-permute-done.8.refs_6_
  67.1 0.6 collective-permute-start.9
  67.7 26.2 %own.2.refs_8_ = f32[4,128,1152]{2,1,0:T(8,128)} custom-call(s32[8,128]{1,0:T(8,128)} %plan.1.table, s32[4]{0:T(128)} %pad_add_fusion.place, bf16[512,2048]{1,0:T(8,128)(2,1)} %bitcast.7.queries, bf16[8192,256]{1,0:T(8,128)(2,1)} %refs_0_.3, bf16[8192,256]{1,0:T(8,128)(2,1)} %refs_1_.3, bf16[8192,256]{1,0:T(8,128)(2,1)} %collective-permute-done.near_keys.refs_2_, ...), custom_call_target="tpu_custom_call" | custom-call | flops 20000000000 | bytes 33554432 | tf_op jit(solution)/shard_map/own/pallas_call | solution.py:396
  93.9 0.0 collective-permute-done.3.refs_1_
  93.9 0.0 collective-permute-done.5.refs_3_
  93.9 0.0 collective-permute-done.7.refs_5_
  94.0 0.0 collective-permute-done.9.refs_7_
  94.0 12.7 %handed.1 = bf16[4,128,2176]{2,1,0:T(8,128)(2,1)} custom-call(s32[8,128]{1,0:T(8,128)} %plan.1.table, s32[4]{0:T(128)} %pad_add_fusion.place, bf16[512,2048]{1,0:T(8,128)(2,1)} %bitcast.7.queries, bf16[2,2048,128]{2,1,0:T(8,128)(2,1)} %collective-permute-done.2.refs_0_, bf16[2,2048,128]{2,1,0:T(8,128)(2,1)} %collective-permute-done.3.refs_1_, ...), custom_call_target="tpu_custom_call" | custom-call | flops 20000000000 | bytes 33554432 | tf_op jit(solution)/shard_map/handed/pallas_call | solution.py:396
  106.7 46.5 %all_to_all.10.parts = bf16[16,32,2176]{2,1,0:T(8,128)(2,1)} all-to-all(bf16[16,32,2176]{2,1,0:T(8,128)(2,1)} %bitcast.10), channel_id=1, replica_groups=mesh['x'=4,'y'=4,'core'=2,'head'=4] {'x','y'}, dimensions={0} | all-to-all | bytes 4456448 | tf_op jit(solution)/shard_map/all_to_all | solution.py:432
  153.2 3.7 %finish.1 = bf16[32,2048]{1,0:T(8,128)(2,1)} custom-call(bf16[16,32,2176]{2,1,0:T(8,128)(2,1)} %all_to_all.10.parts), custom_call_target="tpu_custom_call" | custom-call | tf_op jit(solution)/shard_map/finish/pallas_call | solution.py:435
Async XLA Ops:
  0.0 18.3 %collective-permute-start = (bf16[8192,256]{1,0:T(8,128)(2,1)}, bf16[8192,256]{1,0:T(8,128)(2,1)}, u32[]{:S(2)}, u32[]{:S(2)}) collective-permute-start(bf16[8192,256]{1,0:T(8,128)(2,1)} %refs_0_.3), channel_id=1, source_target_pairs={{0,4},{4,0},{1,5},{5,1},{2,6},{6,2},{3,7},{7,3},{8,12},{12,8},{9,1... | collective-permute-start | bytes 12582920 | tf_op jit(solution)/shard_map/ppermute | solution.py:28
  0.0 18.3 %collective-permute-start.1 = (bf16[8192,256]{1,0:T(8,128)(2,1)}, bf16[8192,256]{1,0:T(8,128)(2,1)}, u32[]{:S(2)}, u32[]{:S(2)}) collective-permute-start(bf16[8192,256]{1,0:T(8,128)(2,1)} %refs_1_.3), channel_id=1, source_target_pairs={{0,4},{4,0},{1,5},{5,1},{2,6},{6,2},{3,7},{7,3},{8,12},{12,8},{9,1... | collective-permute-start | bytes 12582920 | tf_op jit(solution)/shard_map/ppermute | solution.py:28
  3.0 11.9 %copy-start.2 = (s32[4,8,12]{2,1,0:T(8,128)S(1)}, s32[4,8,12]{2,1,0:T(8,128)}, u32[]{:S(2)}) copy-start(s32[4,8,12]{2,1,0:T(8,128)} %param.7) | copy-start | bytes 4612
  3.0 42.2 %all-to-all-start = ((bf16[64,8,2048]{2,1,0:T(8,128)(2,1)}), bf16[64,8,2048]{2,1,0:T(8,128)(2,1)}, u32[]{:S(2)}, u32[]{:S(2)}) async-start(bf16[64,8,2048]{2,1,0:T(8,128)(2,1)} %bitcast.6), calls=%async_computation | async-start | bytes 4194304 | tf_op jit(solution)/shard_map/all_to_all | solution.py:446
  18.3 0.7 copy-start
  19.0 0.6 copy-start.1
  24.5 41.9 %collective-permute-start.2 = (bf16[2,2048,128]{2,1,0:T(8,128)(2,1)}, bf16[2,2048,128]{2,1,0:T(8,128)(2,1)}, u32[]{:S(2)}, u32[]{:S(2)}) collective-permute-start(bf16[2,2048,128]{2,1,0:T(8,128)(2,1)} %get-tuple-element.9), channel_id=1, source_target_pairs={{0,32},{32,64},{64,96},{96,0},{1,33},{33,65},{65,97},{97,1},{2,34}... | collective-permute-start | bytes 3145736 | tf_op jit(solution)/shard_map/ppermute | solution.py:34
  26.4 40.1 %collective-permute-start.4 = (bf16[2,2048,128]{2,1,0:T(8,128)(2,1)}, bf16[2,2048,128]{2,1,0:T(8,128)(2,1)}, u32[]{:S(2)}, u32[]{:S(2)}) collective-permute-start(bf16[2,2048,128]{2,1,0:T(8,128)(2,1)} %get-tuple-element.10), channel_id=1, source_target_pairs={{0,96},{32,0},{64,32},{96,64},{1,97},{33,1},{65,33},{97,65},{2,98}... | collective-permute-start | bytes 3145736 | tf_op jit(solution)/shard_map/ppermute | solution.py:34
  27.9 39.1 %collective-permute-start.6 = (bf16[2,2048,128]{2,1,0:T(8,128)(2,1)}, bf16[2,2048,128]{2,1,0:T(8,128)(2,1)}, u32[]{:S(2)}, u32[]{:S(2)}) collective-permute-start(bf16[2,2048,128]{2,1,0:T(8,128)(2,1)} %get-tuple-element.11), channel_id=1, source_target_pairs={{0,8},{8,16},{16,24},{24,0},{1,9},{9,17},{17,25},{25,1},{2,10},{10... | collective-permute-start | bytes 3145736 | tf_op jit(solution)/shard_map/ppermute | solution.py:34
  29.6 37.5 %collective-permute-start.8 = (bf16[2,2048,128]{2,1,0:T(8,128)(2,1)}, bf16[2,2048,128]{2,1,0:T(8,128)(2,1)}, u32[]{:S(2)}, u32[]{:S(2)}) collective-permute-start(bf16[2,2048,128]{2,1,0:T(8,128)(2,1)} %get-tuple-element.12), channel_id=1, source_target_pairs={{0,24},{8,0},{16,8},{24,16},{1,25},{9,1},{17,9},{25,17},{2,26},{10... | collective-permute-start | bytes 3145736 | tf_op jit(solution)/shard_map/ppermute | solution.py:34
  66.4 27.5 %collective-permute-start.3 = (bf16[2,2048,128]{2,1,0:T(8,128)(2,1)}, bf16[2,2048,128]{2,1,0:T(8,128)(2,1)}, u32[]{:S(2)}, u32[]{:S(2)}) collective-permute-start(bf16[2,2048,128]{2,1,0:T(8,128)(2,1)} %collective-permute-done.2.refs_0_), channel_id=1, source_target_pairs={{0,4},{4,0},{1,5},{5,1},{2,6},{6,2},{3,7},{7,3},{8,12},{12,8},{9,1... | collective-permute-start | bytes 3145736 | tf_op jit(solution)/shard_map/ppermute | solution.py:28
  66.5 27.4 %collective-permute-start.5 = (bf16[2,2048,128]{2,1,0:T(8,128)(2,1)}, bf16[2,2048,128]{2,1,0:T(8,128)(2,1)}, u32[]{:S(2)}, u32[]{:S(2)}) collective-permute-start(bf16[2,2048,128]{2,1,0:T(8,128)(2,1)} %collective-permute-done.4.refs_2_), channel_id=1, source_target_pairs={{0,4},{4,0},{1,5},{5,1},{2,6},{6,2},{3,7},{7,3},{8,12},{12,8},{9,1... | collective-permute-start | bytes 3145736 | tf_op jit(solution)/shard_map/ppermute | solution.py:28
  67.0 27.0 %collective-permute-start.7 = (bf16[2,2048,128]{2,1,0:T(8,128)(2,1)}, bf16[2,2048,128]{2,1,0:T(8,128)(2,1)}, u32[]{:S(2)}, u32[]{:S(2)}) collective-permute-start(bf16[2,2048,128]{2,1,0:T(8,128)(2,1)} %collective-permute-done.6.refs_4_), channel_id=1, source_target_pairs={{0,4},{4,0},{1,5},{5,1},{2,6},{6,2},{3,7},{7,3},{8,12},{12,8},{9,1... | collective-permute-start | bytes 3145736 | tf_op jit(solution)/shard_map/ppermute | solution.py:28
  67.1 26.9 %collective-permute-start.9 = (bf16[2,2048,128]{2,1,0:T(8,128)(2,1)}, bf16[2,2048,128]{2,1,0:T(8,128)(2,1)}, u32[]{:S(2)}, u32[]{:S(2)}) collective-permute-start(bf16[2,2048,128]{2,1,0:T(8,128)(2,1)} %collective-permute-done.8.refs_6_), channel_id=1, source_target_pairs={{0,4},{4,0},{1,5},{5,1},{2,6},{6,2},{3,7},{7,3},{8,12},{12,8},{9,1... | collective-permute-start | bytes 3145736 | tf_op jit(solution)/shard_map/ppermute | solution.py:28
where the time goes:
time: 160 us; the launch traced here: 157 us
  Pallas kernels  70.6 us (44%)
  blocking collectives  46.5 us (29%)
  starting transfers between devices  20.4 us (13%)
  waiting for transfers between devices  14 us (9%)
  local copies, waits for them, and re-layouts  4.53 us (3%)
    pallas_call x3, Pallas kernels, attention(): pl.pallas_call(functools.partial(attention_kernel, base=base, tasks=tasks...  60 us
    all_to_all x1, blocking collectives, finish(): lax.all_to_all(partial.reshape(16, CHUNK, BOTH), ('x', 'y'), split_axis=0...  46.5 us
    all_to_all x1, waiting for transfers between devices, gather(): lax.all_to_all(sent, ('x', 'y', 'head'), split_axis=0, concat_axis=0, til...  14 us
    all_to_all x1, starting transfers between devices, gather(): lax.all_to_all(sent, ('x', 'y', 'head'), split_axis=0, concat_axis=0, til...  11.9 us
    ppermute x4, starting transfers between devices, hand_on(): return lax.ppermute(array, axis, [(i, (i + step) % 4) for i in range(4)])  6.76 us
    pallas_call x1, Pallas kernels, ship(): pl.pallas_call(ship_kernel, in_specs=[pl.BlockSpec(memory_space=pltpu.SME...  4.86 us
    pallas_call x1, Pallas kernels, finish(): pl.pallas_call(finish_kernel, out_shape=jax.ShapeDtypeStruct((CHUNK, 2 *...  3.65 us
  transfers between devices with their start and end apart: 11, of which 1 were waited for; matrix products, arithmetic and copies ran while one was open for 2% of the time, Pallas kernels for 35%

commit v1 on v0

--- a/solution.py
+++ b/solution.py
@@ -19,6 +19,8 @@
 NEG = -1e30
 NT = (((1,), (1,)), ((), ()))
 VMEM = 127 * 2**19
+ROOM = 36 * 2**20
+EARLY, LATER = 4, 6
 HALF = BLOCK // 2
 ARRIVAL = 5
 DIRECTIONS = ((1, 0), (-1, 0), (0, 1), (0, -1))
@@ -26,6 +28,10 @@
 
 def other_core(array):
     return lax.ppermute(array, "core", [(0, 1), (1, 0)])
+
+
+def in_hbm(array):
+    return pltpu.with_memory_space_constraint(array, pltpu.HBM)
 
 
 def hand_on(array, direction):
@@ -146,39 +152,36 @@
     )(table, place, *sources)
 
 
-def attention_kernel(table, place, queries, *refs, base, tasks):
-    handed = tasks == 8
-    if handed:
-        sources, before, refs = refs[:8], refs[8:10], refs[10:]
-    else:
-        sources, refs = refs[:4], refs[4:]
-    out, stacked, peak, total, key_buffer, value_buffer, units, starts, sems = refs
+def attention_kernel(table, place, queries, *refs, first, limit):
+    final = limit is None
+    sources, refs = refs[: 12 if final else 4], refs[12 if final else 4 :]
+    if first:
+        before, refs = refs[0], refs[1:]
+    out, stacked, peak, total, key_buffer, value_buffer, units, starts, touched, sems = refs
     x, y, core = place[0], place[1], place[2]
     lane = lax.broadcasted_iota(jnp.int32, (ROWS, 128), 1)
 
     def copies(unit, slot):
-        code = (units[unit] // 2) % 4
-        head = units[unit] // 8
+        code = (units[unit] // 2) % 8
+        head = units[unit] // 16
         result = []
-        if handed:
-            for d in range(4):
-                group = []
-                for part, buffer in ((0, key_buffer), (1, value_buffer)):
-                    for place_of, source in ((core, sources[2 * d]), (1 - core, sources[2 * d + 1])):
-                        rows = pl.ds(pl.multiple_of(place_of * HALF, HALF), HALF)
-                        sem = sems.at[len(group), slot]
-                        group.append(pltpu.make_async_copy(source.at[part], buffer.at[slot, rows], sem))
-                result.append((code == d, group))
-        else:
-            rows = pl.ds(pl.multiple_of((code % 2) * BLOCK, BLOCK), BLOCK)
-            cols = pl.ds(pl.multiple_of(head * HEAD, HEAD), HEAD)
-            for near in range(2):
-                keys, values = sources[2 * near], sources[2 * near + 1]
-                group = [
-                    pltpu.make_async_copy(keys.at[rows, cols], key_buffer.at[slot], sems.at[0, slot]),
-                    pltpu.make_async_copy(values.at[rows, cols], value_buffer.at[slot], sems.at[1, slot]),
-                ]
-                result.append((code // 2 == near, group))
+        rows = pl.ds(pl.multiple_of((code % 2) * BLOCK, BLOCK), BLOCK)
+        cols = pl.ds(pl.multiple_of(head * HEAD, HEAD), HEAD)
+        for near in range(2):
+            keys, values = sources[2 * near], sources[2 * near + 1]
+            group = [
+                pltpu.make_async_copy(keys.at[rows, cols], key_buffer.at[slot], sems.at[0, slot]),
+                pltpu.make_async_copy(values.at[rows, cols], value_buffer.at[slot], sems.at[1, slot]),
+            ]
+            result.append((code // 2 == near, group))
+        for d in range(4 if final else 0):
+            group = []
+            for part, buffer in ((0, key_buffer), (1, value_buffer)):
+                for half, source in ((core, sources[4 + 2 * d]), (1 - core, sources[5 + 2 * d])):
+                    rows = pl.ds(pl.multiple_of(half * HALF, HALF), HALF)
+                    sem = sems.at[len(group), slot]
+                    group.append(pltpu.make_async_copy(source.at[part], buffer.at[slot, rows], sem))
+            result.append((code == 4 + d, group))
         return result
 
     def start(unit, slot):
@@ -197,59 +200,67 @@
                 for copy in group:
                     copy.wait()
 
-    def list_units(t, count):
+    def list_units(t, carry):
+        count, seen = carry
         starts[t] = count
-        head, q = base + t // 4, t % 4
-        for code in range(4):
-            if handed:
-                dx, dy = DIRECTIONS[code]
+        head, q = t // 4, t % 4
+        seen_before = seen
+        for code in range(8 if final else 4):
+            if code < 4:
+                own = (core if code < 2 else 1 - core) * 2 + code % 2
+                wanted = (table[0, 0] >> (8 * q + 4 * head + own)) & 1
+                block = (x * 4 + y) * 4 + own
+                ours = seen >= first
+                if not final:
+                    ours = jnp.logical_and(ours, seen < limit)
+                seen = seen + wanted
+                wanted = jnp.where(ours, wanted, 0)
+            else:
+                dx, dy = DIRECTIONS[code - 4]
                 giver = ((x - dx + 4) % 4) * 4 + (y - dy + 4) % 4
-                entry = table[0, 5 + code]
+                entry = table[0, 1 + code]
                 item = entry // 16
                 wanted = jnp.where(item // 4 == head, (entry >> q) & 1, 0)
                 block = giver * 4 + item % 4
-            else:
-                own = (core if code < 2 else 1 - core) * 2 + code % 2
-                wanted = (table[0, 0] >> (8 * q + 4 * head + own)) & 1
-                block = (x * 4 + y) * 4 + own
             at = count
 
             @pl.when(wanted != 0)
             def _():
-                units[at] = 8 * head + 2 * code + (block == 63).astype(jnp.int32)
+                units[at] = 16 * head + 2 * code + (block == 63).astype(jnp.int32)
 
             count = count + wanted
-        return count
-
-    starts[tasks] = lax.fori_loop(0, tasks, list_units, 0)
-
-    @pl.when(starts[tasks] > 0)
+        touched[t] = (jnp.minimum(seen, first) > seen_before).astype(jnp.int32)
+        return count, seen
+
+    starts[8] = lax.fori_loop(0, 8, list_units, (0, 0))[0]
+
+    @pl.when(starts[8] > 0)
     def _():
         start(0, 0)
 
     def columns(task, h):
-        first = (base + task // 4) * WIDE + h * HEAD
-        return pl.ds(pl.multiple_of(first, HEAD), HEAD)
-
-    def for_head(task, action):
-        for head in range(2):
-            pl.when(task // 4 == head)(functools.partial(action, before[head].at[task % 4]))
-
-    def load(task, earlier=None):
+        return pl.ds(pl.multiple_of((task // 4) * WIDE + h * HEAD, HEAD), HEAD)
+
+    def load(task):
         tokens = pl.ds(pl.multiple_of((task % 4) * ROWS, ROWS), ROWS)
         for h in range(GROUP):
-            rows = slice(h * ROWS, (h + 1) * ROWS)
-            stacked[rows, :] = queries[tokens, columns(task, h)]
-            if earlier is not None:
-                level = earlier[:, WIDE + 4 * h : WIDE + 4 * h + 1]
-                peak[rows, :] = jnp.broadcast_to(level, (ROWS, HEAD))
-                total[rows, :HEAD] = earlier[:, h * HEAD : (h + 1) * HEAD]
-                total[rows, HEAD:] = jnp.broadcast_to(
-                    jnp.where(level > 0.5 * NEG, 1.0, 0.0), (ROWS, HEAD)
-                )
-        if earlier is None:
+            stacked[h * ROWS : (h + 1) * ROWS, :] = queries[tokens, columns(task, h)]
+
+        @pl.when(touched[task] == 0)
+        def _():
             peak[...] = jnp.full(peak.shape, NEG, jnp.float32)
             total[...] = jnp.zeros(total.shape, jnp.float32)
+
+        if first:
+
+            @pl.when(touched[task] != 0)
+            def _():
+                total[:, HEAD:] = jnp.ones((GROUP * ROWS, HEAD), jnp.float32)
+                for h in range(GROUP):
+                    rows = slice(h * ROWS, (h + 1) * ROWS)
+                    level = before[task, :, WIDE + 4 * h : WIDE + 4 * h + 1]
+                    peak[rows, :] = jnp.broadcast_to(level, (ROWS, HEAD))
+                    total[rows, :HEAD] = before[task, :, h * HEAD : (h + 1) * HEAD]
 
     tile = 2 * ROWS
 
@@ -289,7 +300,7 @@
         slot = unit % 2
         wait(unit, slot)
 
-        @pl.when(unit + 1 < starts[tasks])
+        @pl.when(unit + 1 < starts[8])
         def _():
             start(unit + 1, 1 - slot)
 
@@ -322,28 +333,27 @@
             total[...] = jnp.zeros(total.shape, jnp.float32)
 
     def write(task, h, value):
-        if handed:
+        if final:
             out[task % 4, :, columns(task, h)] = value.astype(jnp.bfloat16)
         else:
-            out[task % 4, :, h * HEAD : (h + 1) * HEAD] = value
+            out[task, :, h * HEAD : (h + 1) * HEAD] = value
 
     def write_levels(task, levels):
+        if not final:
+            out[task, :, WIDE:] = levels
+            return
         q = task % 4
-        if not handed:
-            out[q, :, WIDE:] = levels
-            return
         packed = pack_stats(levels, lane)
         kept = out[q, :, 2 * WIDE :].astype(jnp.float32)
         kept = jnp.where(jnp.logical_and(task >= 4, lane < 32), kept, packed.astype(jnp.float32))
         out[q, :, 2 * WIDE :] = kept.astype(jnp.bfloat16)
 
     def one_task(task, carry):
-        @pl.when(starts[task] < starts[task + 1])
+        some = starts[task] < starts[task + 1]
+
+        @pl.when(some)
         def _():
-            if handed:
-                for_head(task, functools.partial(load, task))
-            else:
-                load(task)
+            load(task)
             lax.fori_loop(starts[task], starts[task + 1], visit, task)
             levels = jnp.full((ROWS, 128), NEG, jnp.float32)
             for h in range(GROUP):
@@ -353,22 +363,25 @@
                 levels = jnp.where((lane % 32) // 4 == h, peak[rows, :] + jnp.log2(mass), levels)
             write_levels(task, levels)
 
-        @pl.when(starts[task] == starts[task + 1])
-        def _():
-            def same(earlier):
+        if first:
+
+            @pl.when(jnp.logical_and(jnp.logical_not(some), touched[task] != 0))
+            def _():
                 for h in range(GROUP):
-                    write(task, h, earlier[:, h * HEAD : (h + 1) * HEAD])
-                write_levels(task, earlier[:, WIDE:])
-
-            if handed:
-                for_head(task, same)
-            else:
-                out[task % 4, :, :WIDE] = jnp.zeros((ROWS, WIDE), jnp.float32)
+                    write(task, h, before[task, :, h * HEAD : (h + 1) * HEAD])
+                write_levels(task, before[task, :, WIDE:])
+
+        if final:
+
+            @pl.when(jnp.logical_and(jnp.logical_not(some), touched[task] == 0))
+            def _():
+                for h in range(GROUP):
+                    write(task, h, jnp.zeros((ROWS, HEAD), jnp.float32))
                 write_levels(task, jnp.full((ROWS, 128), NEG, jnp.float32))
 
         return carry
 
-    lax.fori_loop(0, tasks, one_task, 0)
+    lax.fori_loop(0, 8, one_task, 0)
 
 
 def pack_stats(level, lane):
@@ -385,16 +398,16 @@
     return terms.astype(jnp.bfloat16)
 
 
-def attention(table, place, queries, sources, base, tasks, before=()):
+def attention(table, place, queries, sources, first, limit, before=()):
     smem = pl.BlockSpec(memory_space=pltpu.SMEM)
     vmem = pl.BlockSpec(memory_space=pltpu.VMEM)
     hbm = pl.BlockSpec(memory_space=pl.ANY)
-    if tasks == 8:
+    if limit is None:
         shape = jax.ShapeDtypeStruct((4, ROWS, BOTH), jnp.bfloat16)
     else:
-        shape = jax.ShapeDtypeStruct((4, ROWS, PACK), jnp.float32)
+        shape = jax.ShapeDtypeStruct((8, ROWS, PACK), jnp.float32)
     return pl.pallas_call(
-        functools.partial(attention_kernel, base=base, tasks=tasks),
+        functools.partial(attention_kernel, first=first, limit=limit),
         in_specs=[smem] * 2 + [vmem] + [hbm] * len(sources) + [vmem] * len(before),
         out_specs=vmem,
         out_shape=shape,
@@ -404,13 +417,14 @@
             pltpu.VMEM((GROUP * ROWS, 2 * HEAD), jnp.float32),
             pltpu.VMEM((2, BLOCK, HEAD), jnp.bfloat16),
             pltpu.VMEM((2, BLOCK, HEAD), jnp.bfloat16),
-            pltpu.SMEM((33,), jnp.int32),
+            pltpu.SMEM((65,), jnp.int32),
             pltpu.SMEM((9,), jnp.int32),
+            pltpu.SMEM((8,), jnp.int32),
             pltpu.SemaphoreType.DMA((4, 2)),
         ],
-        compiler_params=pltpu.CompilerParams(vmem_limit_bytes=VMEM),
+        compiler_params=pltpu.CompilerParams(vmem_limit_bytes=ROOM),
         cost_estimate=pl.CostEstimate(flops=2 * 10**10, bytes_accessed=2**25, transcendentals=0),
-        name="handed" if tasks == 8 else "own",
+        name="handed" if limit is None else "own",
     )(table, place, queries, *sources, *before)
 
 
@@ -451,16 +465,16 @@
     place = jnp.stack([lax.axis_index(name) for name in ("x", "y", "core", "head")]).astype(jnp.int32)
     gathered = gather(queries)
     table = plan(gates, place)
-    sources = [keys, values, other_core(keys), other_core(values)]
-    sources = [pltpu.with_memory_space_constraint(source, pltpu.HBM) for source in sources]
+    sources = [in_hbm(a) for a in (keys, values, other_core(keys), other_core(values))]
 
     slots = []
     for d, half in enumerate(ship(table, place, sources)):
         got = hand_on(half, d)
         slots += [got, other_core(got)]
 
-    own = [attention(table, place, gathered, sources, head, 4) for head in range(2)]
-    return finish(attention(table, place, gathered, slots, 0, 8, own))
+    partial = attention(table, place, gathered, sources, 0, EARLY)
+    partial = attention(table, place, gathered, sources, EARLY, LATER, [partial])
+    return finish(attention(table, place, gathered, sources + slots, LATER, None, [partial]))
 
 
 def solution(mesh):

time: 160 us -> 148 us (0.925)
  the two profiles are of different devices: /device:TPU:0 before, /device:TPU:64 now
where the time goes in v1:
time: 148 us; the launch traced here: 145 us
  blocking collectives  62.8 us (42%)
  waiting for transfers between devices  32.5 us (22%)
  Pallas kernels  25.4 us (17%)
  starting transfers between devices  19.2 us (13%)
  local copies, waits for them, and re-layouts  4.47 us (3%)
    all_to_all x1, blocking collectives, finish(): lax.all_to_all(partial.reshape(16, CHUNK, BOTH), ('x', 'y'), split_axis=0...  62.8 us
    ppermute x4, waiting for transfers between devices, hand_on(): return lax.ppermute(array, axis, [(i, (i + step) % 4) for i in range(4)])  16.8 us
    pallas_call x3, Pallas kernels, attention(): pl.pallas_call(functools.partial(attention_kernel, first=first, limit=lim...  13.9 us
    all_to_all x1, waiting for transfers between devices, gather(): lax.all_to_all(sent, ('x', 'y', 'head'), split_axis=0, concat_axis=0, til...  11.9 us
    all_to_all x1, starting transfers between devices, gather(): lax.all_to_all(sent, ('x', 'y', 'head'), split_axis=0, concat_axis=0, til...  10.8 us
    ppermute x4, starting transfers between devices, hand_on(): return lax.ppermute(array, axis, [(i, (i + step) % 4) for i in range(4)])  6.69 us
    pallas_call x1, Pallas kernels, ship(): pl.pallas_call(ship_kernel, in_specs=[pl.BlockSpec(memory_space=pltpu.SME...  5.63 us
    ppermute x6, waiting for transfers between devices, other_core(): return lax.ppermute(array, 'core', [(0, 1), (1, 0)])  3.93 us
  transfers between devices with their start and end apart: 11, of which 5 were waited for; matrix products, arithmetic and copies ran while one was open for 3% of the time, Pallas kernels for 8%

profile of v1, /device:TPU:64, one launch (start us, length us, event | category | flops | bytes accessed | tf_op | source)
XLA Modules:
  0.0 145.3 jit_solution(7692817433056843614)
XLA Ops:
  0.0 0.0 copy-start.4
  0.0 0.0 collective-permute-start
  0.0 0.5 collective-permute-start.1
  0.5 2.5 %broadcast_in_dim.2 = bf16[16,4,8,2048]{3,2,1,0:T(8,128)(2,1)} broadcast(bf16[4,8,2048]{2,1,0:T(8,128)(2,1)} %bitcast.11), dimensions={1,2,3} | broadcast | bytes 2228224 | tf_op jit(solution)/shard_map/broadcast_in_dim | solution.py:459
  3.0 10.8 %all-to-all-start = ((bf16[64,8,2048]{2,1,0:T(8,128)(2,1)}), bf16[64,8,2048]{2,1,0:T(8,128)(2,1)}, u32[]{:S(2)}, u32[]{:S(2)}) async-start(bf16[64,8,2048]{2,1,0:T(8,128)(2,1)} %bitcast.6), calls=%async_computation | async-start | bytes 4194304 | tf_op jit(solution)/shard_map/all_to_all | solution.py:460
  13.8 0.0 copy-done.4
  13.8 0.7 reshape.16.gates
  14.5 0.6 pad_add_fusion.place
  15.1 0.0 copy-start.3
  15.1 2.2 %plan.1.table = s32[8,128]{1,0:T(8,128)} custom-call(s32[384]{0:T(512)} %reshape.16.gates, s32[4]{0:T(128)} %pad_add_fusion.place), custom_call_target="tpu_custom_call" | custom-call | tf_op jit(solution)/shard_map/plan/pallas_call | solution.py:108
  17.3 0.0 collective-permute-done.near_keys.refs_2_
  17.3 0.0 collective-permute-done.1.near_values.refs_3_
  17.3 0.0 copy-start
  17.3 0.7 copy-done
  18.0 0.0 copy-start.2
  18.0 0.6 copy-done.2
  18.6 0.0 copy-start.1
  18.6 5.6 %ship.1 = (bf16[2,2048,128]{2,1,0:T(8,128)(2,1)}, bf16[2,2048,128]{2,1,0:T(8,128)(2,1)}, bf16[2,2048,128]{2,1,0:T(8,128)(2,1)}, bf16[2,2048,128]{2,1,0:T(8,128)(2,1)}) custom-call(s32[8,128]{1,0:T(8,128)S(1)} %copy-done, s32[4]{0:T(128)S(1)} %copy-done.2, bf16[8192,256]{1,0:T(8,128)(2,1)} %refs_0_.5, bf16[8192,256]{1,0:T(8,128)(2,1)} %refs_1_.5, ...), custom_call_target="tpu_custom_call" | custom-call | bytes 1024 | tf_op jit(solution)/shard_map/ship/pallas_call | solution.py:143
  24.2 1.5 %collective-permute-start.2 = (bf16[2,2048,128]{2,1,0:T(8,128)(2,1)}, bf16[2,2048,128]{2,1,0:T(8,128)(2,1)S(1)}, u32[]{:S(2)}, u32[]{:S(2)}) collective-permute-start(bf16[2,2048,128]{2,1,0:T(8,128)(2,1)} %get-tuple-element.9), channel_id=1, source_target_pairs={{0,32},{32,64},{64,96},{96,0},{1,33},{33,65},{65,97},{97,1},{2,34}... | collective-permute-start | bytes 3145736 | tf_op jit(solution)/shard_map/ppermute | solution.py:40
  25.8 1.8 %collective-permute-start.4 = (bf16[2,2048,128]{2,1,0:T(8,128)(2,1)}, bf16[2,2048,128]{2,1,0:T(8,128)(2,1)S(1)}, u32[]{:S(2)}, u32[]{:S(2)}) collective-permute-start(bf16[2,2048,128]{2,1,0:T(8,128)(2,1)} %get-tuple-element.10), channel_id=1, source_target_pairs={{0,96},{32,0},{64,32},{96,64},{1,97},{33,1},{65,33},{97,65},{2,98}... | collective-permute-start | bytes 3145736 | tf_op jit(solution)/shard_map/ppermute | solution.py:40
  27.5 1.2 collective-permute-start.6
  28.8 2.2 %collective-permute-start.8 = (bf16[2,2048,128]{2,1,0:T(8,128)(2,1)}, bf16[2,2048,128]{2,1,0:T(8,128)(2,1)}, u32[]{:S(2)}, u32[]{:S(2)}) collective-permute-start(bf16[2,2048,128]{2,1,0:T(8,128)(2,1)} %get-tuple-element.12), channel_id=1, source_target_pairs={{0,24},{8,0},{16,8},{24,16},{1,25},{9,1},{17,9},{25,17},{2,26},{10... | collective-permute-start | bytes 3145736 | tf_op jit(solution)/shard_map/ppermute | solution.py:40
  30.9 11.9 %all-to-all-done = bf16[64,8,2048]{2,1,0:T(8,128)(2,1)} async-done(((bf16[64,8,2048]{2,1,0:T(8,128)(2,1)}), bf16[64,8,2048]{2,1,0:T(8,128)(2,1)}, u32[]{:S(2)}, u32[]{:S(2)}) %all-to-all-start) | async-done | bytes 2097184 | tf_op jit(solution)/shard_map/all_to_all | solution.py:460
  42.8 0.0 copy-done.3
  42.8 0.0 copy-done.1
  42.8 2.1 %own.2.refs_4_ = f32[8,128,1152]{2,1,0:T(8,128)S(1)} custom-call(s32[8,128]{1,0:T(8,128)S(1)} %copy-done.1, s32[4]{0:T(128)S(1)} %copy-done.3, bf16[512,2048]{1,0:T(8,128)(2,1)} %bitcast.7.queries, bf16[8192,256]{1,0:T(8,128)(2,1)} %refs_0_.5, bf16[8192,256]{1,0:T(8,128)(2,1)} %refs_1_.5, bf16[8192,256]{1,0:T(8,128)(2,1)} %collective-permute-done.near_keys.refs_2_, ...), custom_call_target="tpu_custom_call" | custom-call | flops 20000000000 | bytes 33554432 | tf_op jit(solution)/shard_map/own/pallas_call | solution.py:409
  44.9 16.8 %collective-permute-done.2.refs_4_ = bf16[2,2048,128]{2,1,0:T(8,128)(2,1)S(1)} collective-permute-done((bf16[2,2048,128]{2,1,0:T(8,128)(2,1)}, bf16[2,2048,128]{2,1,0:T(8,128)(2,1)S(1)}, u32[]{:S(2)}, u32[]{:S(2)}) %collective-permute-start.2) | collective-permute-done | bytes 1048608 | tf_op jit(solution)/shard_map/ppermute | solution.py:40
  61.7 0.0 collective-permute-start.3
  61.7 0.0 collective-permute-done.4.refs_6_
  61.7 0.5 collective-permute-start.5
  62.2 0.0 collective-permute-done.6.refs_8_
  62.2 0.1 collective-permute-start.7
  62.3 0.0 collective-permute-done.8.refs_10_
  62.3 0.6 collective-permute-start.9
  62.9 2.2 %own.3.refs_12_ = f32[8,128,1152]{2,1,0:T(8,128)S(1)} custom-call(s32[8,128]{1,0:T(8,128)S(1)} %copy-done.1, s32[4]{0:T(128)S(1)} %copy-done.3, bf16[512,2048]{1,0:T(8,128)(2,1)} %bitcast.7.queries, bf16[8192,256]{1,0:T(8,128)(2,1)} %refs_0_.5, bf16[8192,256]{1,0:T(8,128)(2,1)} %refs_1_.5, bf16[8192,256]{1,0:T(8,128)(2,1)} %collective-permute-done.near_keys.refs_2_, ...), custom_call_target="tpu_custom_call" | custom-call | flops 20000000000 | bytes 33554432 | tf_op jit(solution)/shard_map/own/pallas_call | solution.py:409
  65.1 0.0 collective-permute-done.3.refs_5_
  65.1 2.2 %collective-permute-done.5.refs_7_ = bf16[2,2048,128]{2,1,0:T(8,128)(2,1)S(1)} collective-permute-done((bf16[2,2048,128]{2,1,0:T(8,128)(2,1)S(1)}, bf16[2,2048,128]{2,1,0:T(8,128)(2,1)S(1)}, u32[]{:S(2)}, u32[]{:S(2)}) %collective-permute-start.5) | collective-permute-done | bytes 1048608 | tf_op jit(solution)/shard_map/ppermute | solution.py:30
  67.3 0.2 collective-permute-done.7.refs_9_
  67.5 1.5 %collective-permute-done.9.refs_11_ = bf16[2,2048,128]{2,1,0:T(8,128)(2,1)S(1)} collective-permute-done((bf16[2,2048,128]{2,1,0:T(8,128)(2,1)}, bf16[2,2048,128]{2,1,0:T(8,128)(2,1)S(1)}, u32[]{:S(2)}, u32[]{:S(2)}) %collective-permute-start.9) | collective-permute-done | bytes 1048608 | tf_op jit(solution)/shard_map/ppermute | solution.py:30
  69.0 9.6 %handed.1 = bf16[4,128,2176]{2,1,0:T(8,128)(2,1)S(1)} custom-call(s32[8,128]{1,0:T(8,128)S(1)} %copy-done.1, s32[4]{0:T(128)S(1)} %copy-done.3, bf16[512,2048]{1,0:T(8,128)(2,1)} %bitcast.7.queries, bf16[8192,256]{1,0:T(8,128)(2,1)} %refs_0_.5, bf16[8192,256]{1,0:T(8,128)(2,1)} %refs_1_.5, bf16[8192,256]{1,0:T(8,128)(2,1)} %collective-permute-done.near_keys.refs_2_, ...), custom_call_target="tpu_custom_call" | custom-call | flops 20000000000 | bytes 33554432 | tf_op jit(solution)/shard_map/handed/pallas_call | solution.py:409
  78.7 62.8 %all_to_all.10.parts = bf16[16,32,2176]{2,1,0:T(8,128)(2,1)} all-to-all(bf16[16,32,2176]{2,1,0:T(8,128)(2,1)S(1)} %bitcast.10), channel_id=1, replica_groups=mesh['x'=4,'y'=4,'core'=2,'head'=4] {'x','y'}, dimensions={0} | all-to-all | bytes 4456448 | tf_op jit(solution)/shard_map/all_to_all | solution.py:446
  141.4 3.7 %finish.1 = bf16[32,2048]{1,0:T(8,128)(2,1)} custom-call(bf16[16,32,2176]{2,1,0:T(8,128)(2,1)} %all_to_all.10.parts), custom_call_target="tpu_custom_call" | custom-call | tf_op jit(solution)/shard_map/finish/pallas_call | solution.py:449
Async XLA Ops:
  0.0 13.8 %copy-start.4 = (s32[4,8,12]{2,1,0:T(8,128)S(1)}, s32[4,8,12]{2,1,0:T(8,128)}, u32[]{:S(2)}) copy-start(s32[4,8,12]{2,1,0:T(8,128)} %param.7) | copy-start | bytes 4612
  0.0 17.3 %collective-permute-start = (bf16[8192,256]{1,0:T(8,128)(2,1)}, bf16[8192,256]{1,0:T(8,128)(2,1)}, u32[]{:S(2)}, u32[]{:S(2)}) collective-permute-start(bf16[8192,256]{1,0:T(8,128)(2,1)} %refs_0_.5), channel_id=1, source_target_pairs={{0,4},{4,0},{1,5},{5,1},{2,6},{6,2},{3,7},{7,3},{8,12},{12,8},{9,1... | collective-permute-start | bytes 12582920 | tf_op jit(solution)/shard_map/ppermute | solution.py:30
  0.0 17.3 %collective-permute-start.1 = (bf16[8192,256]{1,0:T(8,128)(2,1)}, bf16[8192,256]{1,0:T(8,128)(2,1)}, u32[]{:S(2)}, u32[]{:S(2)}) collective-permute-start(bf16[8192,256]{1,0:T(8,128)(2,1)} %refs_1_.5), channel_id=1, source_target_pairs={{0,4},{4,0},{1,5},{5,1},{2,6},{6,2},{3,7},{7,3},{8,12},{12,8},{9,1... | collective-permute-start | bytes 12582920 | tf_op jit(solution)/shard_map/ppermute | solution.py:30
  3.0 39.8 %all-to-all-start = ((bf16[64,8,2048]{2,1,0:T(8,128)(2,1)}), bf16[64,8,2048]{2,1,0:T(8,128)(2,1)}, u32[]{:S(2)}, u32[]{:S(2)}) async-start(bf16[64,8,2048]{2,1,0:T(8,128)(2,1)} %bitcast.6), calls=%async_computation | async-start | bytes 4194304 | tf_op jit(solution)/shard_map/all_to_all | solution.py:460
  15.1 27.7 %copy-start.3 = (s32[4]{0:T(128)S(1)}, s32[4]{0:T(128)}, u32[]{:S(2)}) copy-start(s32[4]{0:T(128)} %pad_add_fusion.place) | copy-start | bytes 52
  17.3 0.7 copy-start
  18.0 0.6 copy-start.2
  18.6 24.2 %copy-start.1 = (s32[8,128]{1,0:T(8,128)S(1)}, s32[8,128]{1,0:T(8,128)}, u32[]{:S(2)}) copy-start(s32[8,128]{1,0:T(8,128)} %plan.1.table) | copy-start | bytes 12292
  24.2 37.4 %collective-permute-start.2 = (bf16[2,2048,128]{2,1,0:T(8,128)(2,1)}, bf16[2,2048,128]{2,1,0:T(8,128)(2,1)S(1)}, u32[]{:S(2)}, u32[]{:S(2)}) collective-permute-start(bf16[2,2048,128]{2,1,0:T(8,128)(2,1)} %get-tuple-element.9), channel_id=1, source_target_pairs={{0,32},{32,64},{64,96},{96,0},{1,33},{33,65},{65,97},{97,1},{2,34}... | collective-permute-start | bytes 3145736 | tf_op jit(solution)/shard_map/ppermute | solution.py:40
  25.8 35.9 %collective-permute-start.4 = (bf16[2,2048,128]{2,1,0:T(8,128)(2,1)}, bf16[2,2048,128]{2,1,0:T(8,128)(2,1)S(1)}, u32[]{:S(2)}, u32[]{:S(2)}) collective-permute-start(bf16[2,2048,128]{2,1,0:T(8,128)(2,1)} %get-tuple-element.10), channel_id=1, source_target_pairs={{0,96},{32,0},{64,32},{96,64},{1,97},{33,1},{65,33},{97,65},{2,98}... | collective-permute-start | bytes 3145736 | tf_op jit(solution)/shard_map/ppermute | solution.py:40
  27.5 34.6 %collective-permute-start.6 = (bf16[2,2048,128]{2,1,0:T(8,128)(2,1)}, bf16[2,2048,128]{2,1,0:T(8,128)(2,1)}, u32[]{:S(2)}, u32[]{:S(2)}) collective-permute-start(bf16[2,2048,128]{2,1,0:T(8,128)(2,1)} %get-tuple-element.11), channel_id=1, source_target_pairs={{0,8},{8,16},{16,24},{24,0},{1,9},{9,17},{17,25},{25,1},{2,10},{10... | collective-permute-start | bytes 3145736 | tf_op jit(solution)/shard_map/ppermute | solution.py:40
  28.8 33.5 %collective-permute-start.8 = (bf16[2,2048,128]{2,1,0:T(8,128)(2,1)}, bf16[2,2048,128]{2,1,0:T(8,128)(2,1)}, u32[]{:S(2)}, u32[]{:S(2)}) collective-permute-start(bf16[2,2048,128]{2,1,0:T(8,128)(2,1)} %get-tuple-element.12), channel_id=1, source_target_pairs={{0,24},{8,0},{16,8},{24,16},{1,25},{9,1},{17,9},{25,17},{2,26},{10... | collective-permute-start | bytes 3145736 | tf_op jit(solution)/shard_map/ppermute | solution.py:40
  61.7 3.4 %collective-permute-start.3 = (bf16[2,2048,128]{2,1,0:T(8,128)(2,1)S(1)}, bf16[2,2048,128]{2,1,0:T(8,128)(2,1)S(1)}, u32[]{:S(2)}, u32[]{:S(2)}) collective-permute-start(bf16[2,2048,128]{2,1,0:T(8,128)(2,1)S(1)} %collective-permute-done.2.refs_4_), channel_id=1, source_target_pairs={{0,4},{4,0},{1,5},{5,1},{2,6},{6,2},{3,7},{7,3},{8,12},{12,8},{9,1... | collective-permute-start | bytes 3145736 | tf_op jit(solution)/shard_map/ppermute | solution.py:30
  61.7 5.7 %collective-permute-start.5 = (bf16[2,2048,128]{2,1,0:T(8,128)(2,1)S(1)}, bf16[2,2048,128]{2,1,0:T(8,128)(2,1)S(1)}, u32[]{:S(2)}, u32[]{:S(2)}) collective-permute-start(bf16[2,2048,128]{2,1,0:T(8,128)(2,1)S(1)} %collective-permute-done.4.refs_6_), channel_id=1, source_target_pairs={{0,4},{4,0},{1,5},{5,1},{2,6},{6,2},{3,7},{7,3},{8,12},{12,8},{9,1... | collective-permute-start | bytes 3145736 | tf_op jit(solution)/shard_map/ppermute | solution.py:30
  62.2 5.4 %collective-permute-start.7 = (bf16[2,2048,128]{2,1,0:T(8,128)(2,1)}, bf16[2,2048,128]{2,1,0:T(8,128)(2,1)S(1)}, u32[]{:S(2)}, u32[]{:S(2)}) collective-permute-start(bf16[2,2048,128]{2,1,0:T(8,128)(2,1)} %collective-permute-done.6.refs_8_), channel_id=1, source_target_pairs={{0,4},{4,0},{1,5},{5,1},{2,6},{6,2},{3,7},{7,3},{8,12},{12,8},{9,1... | collective-permute-start | bytes 3145736 | tf_op jit(solution)/shard_map/ppermute | solution.py:30
  62.3 6.8 %collective-permute-start.9 = (bf16[2,2048,128]{2,1,0:T(8,128)(2,1)}, bf16[2,2048,128]{2,1,0:T(8,128)(2,1)S(1)}, u32[]{:S(2)}, u32[]{:S(2)}) collective-permute-start(bf16[2,2048,128]{2,1,0:T(8,128)(2,1)} %collective-permute-done.8.refs_10_), channel_id=1, source_target_pairs={{0,4},{4,0},{1,5},{5,1},{2,6},{6,2},{3,7},{7,3},{8,12},{12,8},{9,1... | collective-permute-start | bytes 3145736 | tf_op jit(solution)/shard_map/ppermute | solution.py:30

commit v2 on v1

--- a/solution.py
+++ b/solution.py
@@ -20,7 +20,7 @@
 NT = (((1,), (1,)), ((), ()))
 VMEM = 127 * 2**19
 ROOM = 36 * 2**20
-EARLY, LATER = 4, 6
+EARLY, LATER = 3, 5
 HALF = BLOCK // 2
 ARRIVAL = 5
 DIRECTIONS = ((1, 0), (-1, 0), (0, 1), (0, -1))
@@ -40,29 +40,30 @@
     return lax.ppermute(array, axis, [(i, (i + step) % 4) for i in range(4)])
 
 
-def plan_kernel(gates, place, table):
+def plan_kernel(gates, table):
     lane = lax.broadcasted_iota(jnp.int32, (8, 128), 1)
     item = lax.broadcasted_iota(jnp.int32, (8, 128), 0)
+    variant = lane // 16
     chip = lane % 16
-    y = chip % 4
+    x, y = chip // 4, chip % 4
     block = chip * 4 + item % 4
-    first = place[3] * 2
+    here_x, here_y, core = (lax.axis_index(name) for name in ("x", "y", "core"))
+    first = lax.axis_index("head") * 2
     kept = []
     for q in range(4):
         hit = jnp.zeros((8, 128), jnp.int32)
         for k in range(12):
-            chosen = jnp.where(item < 4, gates[q * 96 + first * 12 + k], gates[q * 96 + first * 12 + 12 + k])
+            chosen = jnp.where(item < 4, gates[q, first, k], gates[q, first + 1, k])
             hit = jnp.where(chosen == block, 1, hit)
         kept.append(hit)
 
-    def ahead(value, d):
-        if d == 0:
-            return pltpu.roll(value, 124, 1)
-        if d == 1:
-            return pltpu.roll(value, 4, 1)
-        if d == 2:
-            return jnp.where(y < 3, pltpu.roll(value, 127, 1), pltpu.roll(value, 3, 1))
-        return jnp.where(y > 0, pltpu.roll(value, 1, 1), pltpu.roll(value, 125, 1))
+    def ahead(value, direction):
+        forward = jnp.where(x < 3, pltpu.roll(value, 124, 1), pltpu.roll(value, 12, 1))
+        back = jnp.where(x > 0, pltpu.roll(value, 4, 1), pltpu.roll(value, 116, 1))
+        up = jnp.where(y < 3, pltpu.roll(value, 127, 1), pltpu.roll(value, 3, 1))
+        down = jnp.where(y > 0, pltpu.roll(value, 1, 1), pltpu.roll(value, 125, 1))
+        along_x = jnp.where(direction == 0, forward, back)
+        return jnp.where(direction < 2, along_x, jnp.where(direction == 2, up, down))
 
     def over_items(value, how):
         for step in (4, 2, 1):
@@ -71,11 +72,15 @@
 
     own = over_items(kept[0] + kept[1] + kept[2] + kept[3], jnp.add)
     handed = jnp.zeros((8, 128), jnp.int32)
-    given, got = [], []
-    for d in range(4):
+    given = [jnp.zeros((8, 128), jnp.int32)] * 4
+    got = [jnp.zeros((8, 128), jnp.int32)] * 4
+    for orders in zip((0, 1, 2, 3), (2, 3, 0, 1), (0, 2, 1, 3), (3, 1, 2, 0)):
+        direction = jnp.zeros((8, 128), jnp.int32)
+        for i, d in enumerate(orders):
+            direction = jnp.where(variant // 2 == i, d, direction)
         ready = jnp.maximum(own, ARRIVAL) + handed
         done = jnp.where(handed > 0, ready, own)
-        want = jnp.maximum(done - ahead(ready, d), 0) >> 1
+        want = jnp.maximum(done - ahead(ready, direction) + variant % 2, 0) >> 1
         left = kept[0] + kept[1] + kept[2] + kept[3]
         moved = jnp.minimum(left, want)
         score = moved * 256 - left * 16 + item
@@ -90,33 +95,42 @@
             entry = entry + goes * (1 << q)
         moved = over_items(moved, jnp.add)
         entry = over_items(entry, jnp.add)
-        given.append(entry)
-        got.append(ahead(entry, d ^ 1))
+        gets = ahead(entry, direction ^ 1)
+        for d in range(4):
+            given[d] = jnp.where(direction == d, entry, given[d])
+            got[d] = jnp.where(direction == d, gets, got[d])
         own = own - moved
-        handed = handed + ahead(moved, d ^ 1)
+        handed = handed + ahead(moved, direction ^ 1)
+    worst = jnp.where(handed > 0, jnp.maximum(own, ARRIVAL) + handed, own)
+    for step in (8, 4, 2, 1):
+        around = jnp.where(chip + step < 16, pltpu.roll(worst, 128 - step, 1), pltpu.roll(worst, 16 - step, 1))
+        worst = jnp.maximum(worst, around)
+    best = jnp.min((worst * 8 + variant).astype(jnp.float32)).astype(jnp.int32) % 8
+    here = best * 16 + here_x * 4 + here_y
     keeps = jnp.zeros((8, 128), jnp.int32)
     for q in range(4):
         keeps = keeps + (kept[q] << (8 * q + item))
     row = jnp.zeros((8, 128), jnp.int32)
-    here = place[0] * 4 + place[1]
     for i, value in enumerate([over_items(keeps, jnp.add)] + given + got):
         row = jnp.where(lane == i, pltpu.roll(value, (i + 128 - here) % 128, 1), row)
+    for i, value in enumerate((here_x, here_y, core)):
+        row = jnp.where(lane == 9 + i, value, row)
     table[...] = row
 
 
-def plan(gates, place):
+def plan(gates):
     return pl.pallas_call(
         plan_kernel,
-        in_specs=[pl.BlockSpec(memory_space=pltpu.SMEM)] * 2,
+        in_specs=[pl.BlockSpec(memory_space=pltpu.SMEM)],
         out_shape=jax.ShapeDtypeStruct((8, 128), jnp.int32),
         compiler_params=pltpu.CompilerParams(vmem_limit_bytes=VMEM),
         name="plan",
-    )(gates.reshape(-1), place)
-
-
-def ship_kernel(table, place, keys, values, near_keys, near_values, *refs):
+    )(gates)
+
+
+def ship_kernel(table, keys, values, near_keys, near_values, *refs):
     outs, sems = refs[:4], refs[4]
-    core = place[2]
+    core = table[0, 11]
     for phase in range(2):
         for d in range(4):
             item = table[0, 1 + d] // 16
@@ -138,27 +152,27 @@
                             copy.wait()
 
 
-def ship(table, place, sources):
+def ship(table, sources):
     hbm = pl.BlockSpec(memory_space=pl.ANY)
     return pl.pallas_call(
         ship_kernel,
-        in_specs=[pl.BlockSpec(memory_space=pltpu.SMEM)] * 2 + [hbm] * 4,
+        in_specs=[pl.BlockSpec(memory_space=pltpu.SMEM)] + [hbm] * 4,
         out_specs=[pl.BlockSpec(memory_space=pltpu.VMEM)] * 4,
         out_shape=[jax.ShapeDtypeStruct((2, HALF, HEAD), jnp.bfloat16)] * 4,
         scratch_shapes=[pltpu.SemaphoreType.DMA((4, 2))],
         cost_estimate=pl.CostEstimate(flops=0, bytes_accessed=2**10, transcendentals=0),
         compiler_params=pltpu.CompilerParams(vmem_limit_bytes=VMEM // 2),
         name="ship",
-    )(table, place, *sources)
-
-
-def attention_kernel(table, place, queries, *refs, first, limit):
+    )(table, *sources)
+
+
+def attention_kernel(table, queries, *refs, first, limit):
     final = limit is None
     sources, refs = refs[: 12 if final else 4], refs[12 if final else 4 :]
     if first:
         before, refs = refs[0], refs[1:]
     out, stacked, peak, total, key_buffer, value_buffer, units, starts, touched, sems = refs
-    x, y, core = place[0], place[1], place[2]
+    x, y, core = table[0, 9], table[0, 10], table[0, 11]
     lane = lax.broadcasted_iota(jnp.int32, (ROWS, 128), 1)
 
     def copies(unit, slot):
@@ -398,7 +412,7 @@
     return terms.astype(jnp.bfloat16)
 
 
-def attention(table, place, queries, sources, first, limit, before=()):
+def attention(table, queries, sources, first, limit, before=()):
     smem = pl.BlockSpec(memory_space=pltpu.SMEM)
     vmem = pl.BlockSpec(memory_space=pltpu.VMEM)
     hbm = pl.BlockSpec(memory_space=pl.ANY)
@@ -408,7 +422,7 @@
         shape = jax.ShapeDtypeStruct((8, ROWS, PACK), jnp.float32)
     return pl.pallas_call(
         functools.partial(attention_kernel, first=first, limit=limit),
-        in_specs=[smem] * 2 + [vmem] + [hbm] * len(sources) + [vmem] * len(before),
+        in_specs=[smem, vmem] + [hbm] * len(sources) + [vmem] * len(before),
         out_specs=vmem,
         out_shape=shape,
         scratch_shapes=[
@@ -425,7 +439,7 @@
         compiler_params=pltpu.CompilerParams(vmem_limit_bytes=ROOM),
         cost_estimate=pl.CostEstimate(flops=2 * 10**10, bytes_accessed=2**25, transcendentals=0),
         name="handed" if limit is None else "own",
-    )(table, place, queries, *sources, *before)
+    )(table, queries, *sources, *before)
 
 
 def finish_kernel(parts, out):
@@ -462,19 +476,18 @@
 
 
 def shards(queries, keys, values, gates):
-    place = jnp.stack([lax.axis_index(name) for name in ("x", "y", "core", "head")]).astype(jnp.int32)
     gathered = gather(queries)
-    table = plan(gates, place)
+    table = plan(gates)
     sources = [in_hbm(a) for a in (keys, values, other_core(keys), other_core(values))]
 
     slots = []
-    for d, half in enumerate(ship(table, place, sources)):
+    for d, half in enumerate(ship(table, sources)):
         got = hand_on(half, d)
         slots += [got, other_core(got)]
 
-    partial = attention(table, place, gathered, sources, 0, EARLY)
-    partial = attention(table, place, gathered, sources, EARLY, LATER, [partial])
-    return finish(attention(table, place, gathered, sources + slots, LATER, None, [partial]))
+    partial = attention(table, gathered, sources, 0, EARLY)
+    partial = attention(table, gathered, sources, EARLY, LATER, [partial])
+    return finish(attention(table, gathered, sources + slots, LATER, None, [partial]))
 
 
 def solution(mesh):

time: 148 us -> 148 us (level)
  Pallas kernels: 25.4 us -> 42.7 us
  blocking collectives: 62.8 us -> 47.5 us
    pallas_call x3, Pallas kernels: 13.9 us -> 30.7 us  [attention(): pl.pallas_call(functools.partial(attention_kernel, first=first, limit=lim...]
    all_to_all x1, blocking collectives: 62.8 us -> 47.5 us  [finish(): lax.all_to_all(partial.reshape(16, CHUNK, BOTH), ('x', 'y'), split_axis=0...]
  transfers between devices with their start and end apart: 11 -> 11, of which waited for: 5 -> 4; matrix products, arithmetic and copies ran while one was open for 3% -> 2% of each run, Pallas kernels for 8% -> 9%
where the time goes in v2:
time: 148 us; the launch traced here: 146 us
  blocking collectives  47.5 us (32%)
  Pallas kernels  42.7 us (29%)
  waiting for transfers between devices  33.4 us (23%)
  starting transfers between devices  19.4 us (13%)
  local copies, waits for them, and re-layouts  3.17 us (2%)
    all_to_all x1, blocking collectives, finish(): lax.all_to_all(partial.reshape(16, CHUNK, BOTH), ('x', 'y'), split_axis=0...  47.5 us
    pallas_call x3, Pallas kernels, attention(): pl.pallas_call(functools.partial(attention_kernel, first=first, limit=lim...  30.7 us
    ppermute x4, waiting for transfers between devices, hand_on(): return lax.ppermute(array, axis, [(i, (i + step) % 4) for i in range(4)])  16.7 us
    all_to_all x1, waiting for transfers between devices, gather(): lax.all_to_all(sent, ('x', 'y', 'head'), split_axis=0, concat_axis=0, til...  13.2 us
    all_to_all x1, starting transfers between devices, gather(): lax.all_to_all(sent, ('x', 'y', 'head'), split_axis=0, concat_axis=0, til...  10.8 us
    ppermute x4, starting transfers between devices, hand_on(): return lax.ppermute(array, axis, [(i, (i + step) % 4) for i in range(4)])  6.7 us
    pallas_call x1, Pallas kernels, ship(): pl.pallas_call(ship_kernel, in_specs=[pl.BlockSpec(memory_space=pltpu.SME...  5.6 us
    pallas_call x1, Pallas kernels, finish(): pl.pallas_call(finish_kernel, out_shape=jax.ShapeDtypeStruct((CHUNK, 2 *...  3.65 us
  transfers between devices with their start and end apart: 11, of which 4 were waited for; matrix products, arithmetic and copies ran while one was open for 2% of the time, Pallas kernels for 9%

profile of v2, /device:TPU:64, one launch (start us, length us, event | category | flops | bytes accessed | tf_op | source)
XLA Modules:
  0.0 146.4 jit_solution(10186861648423038545)
XLA Ops:
  0.0 0.0 collective-permute-start
  0.0 0.5 collective-permute-start.1
  0.5 2.5 %broadcast_in_dim.2 = bf16[16,4,8,2048]{3,2,1,0:T(8,128)(2,1)} broadcast(bf16[4,8,2048]{2,1,0:T(8,128)(2,1)} %bitcast.7), dimensions={1,2,3} | broadcast | bytes 2228224 | tf_op jit(solution)/shard_map/broadcast_in_dim | solution.py:473
  3.0 10.8 %all-to-all-start = ((bf16[64,8,2048]{2,1,0:T(8,128)(2,1)}), bf16[64,8,2048]{2,1,0:T(8,128)(2,1)}, u32[]{:S(2)}, u32[]{:S(2)}) async-start(bf16[64,8,2048]{2,1,0:T(8,128)(2,1)} %bitcast.2), calls=%async_computation | async-start | bytes 4194304 | tf_op jit(solution)/shard_map/all_to_all | solution.py:474
  13.8 2.8 %plan.1.table = s32[8,128]{1,0:T(8,128)} custom-call(s32[4,8,12]{2,1,0:T(8,128)} %gates.1), custom_call_target="tpu_custom_call" | custom-call | tf_op jit(solution)/shard_map/plan/pallas_call | solution.py:122
  16.6 0.0 collective-permute-done.near_keys.refs_2_
  16.6 0.0 collective-permute-done.1.near_values.refs_3_
  16.6 0.0 copy-start
  16.6 0.7 copy-done
  17.3 0.0 copy-start.1
  17.3 5.6 %ship.1 = (bf16[2,2048,128]{2,1,0:T(8,128)(2,1)}, bf16[2,2048,128]{2,1,0:T(8,128)(2,1)}, bf16[2,2048,128]{2,1,0:T(8,128)(2,1)}, bf16[2,2048,128]{2,1,0:T(8,128)(2,1)}) custom-call(s32[8,128]{1,0:T(8,128)S(1)} %copy-done, bf16[8192,256]{1,0:T(8,128)(2,1)} %refs_0_.5, bf16[8192,256]{1,0:T(8,128)(2,1)} %refs_1_.5, ...), custom_call_target="tpu_custom_call" | custom-call | bytes 1024 | tf_op jit(solution)/shard_map/ship/pallas_call | solution.py:157
  22.9 0.7 collective-permute-start.2
  23.6 2.6 %collective-permute-start.4 = (bf16[2,2048,128]{2,1,0:T(8,128)(2,1)}, bf16[2,2048,128]{2,1,0:T(8,128)(2,1)S(1)}, u32[]{:S(2)}, u32[]{:S(2)}) collective-permute-start(bf16[2,2048,128]{2,1,0:T(8,128)(2,1)} %get-tuple-element.10), channel_id=1, source_target_pairs={{0,96},{32,0},{64,32},{96,64},{1,97},{33,1},{65,33},{97,65},{2,98}... | collective-permute-start | bytes 3145736 | tf_op jit(solution)/shard_map/ppermute | solution.py:40
  26.2 0.7 collective-permute-start.6
  27.0 2.6 %collective-permute-start.8 = (bf16[2,2048,128]{2,1,0:T(8,128)(2,1)}, bf16[2,2048,128]{2,1,0:T(8,128)(2,1)}, u32[]{:S(2)}, u32[]{:S(2)}) collective-permute-start(bf16[2,2048,128]{2,1,0:T(8,128)(2,1)} %get-tuple-element.12), channel_id=1, source_target_pairs={{0,24},{8,0},{16,8},{24,16},{1,25},{9,1},{17,9},{25,17},{2,26},{10... | collective-permute-start | bytes 3145736 | tf_op jit(solution)/shard_map/ppermute | solution.py:40
  29.6 13.2 %all-to-all-done = bf16[64,8,2048]{2,1,0:T(8,128)(2,1)} async-done(((bf16[64,8,2048]{2,1,0:T(8,128)(2,1)}), bf16[64,8,2048]{2,1,0:T(8,128)(2,1)}, u32[]{:S(2)}, u32[]{:S(2)}) %all-to-all-start) | async-done | bytes 2097184 | tf_op jit(solution)/shard_map/all_to_all | solution.py:474
  42.8 0.0 copy-done.1
  42.8 2.1 %own.2.refs_4_ = f32[8,128,1152]{2,1,0:T(8,128)S(1)} custom-call(s32[8,128]{1,0:T(8,128)S(1)} %copy-done.1, bf16[512,2048]{1,0:T(8,128)(2,1)} %bitcast.3.queries, bf16[8192,256]{1,0:T(8,128)(2,1)} %refs_0_.5, bf16[8192,256]{1,0:T(8,128)(2,1)} %refs_1_.5, bf16[8192,256]{1,0:T(8,128)(2,1)} %collective-permute-done.near_keys.refs_2_, ...), custom_call_target="tpu_custom_call" | custom-call | flops 20000000000 | bytes 33554432 | tf_op jit(solution)/shard_map/own/pallas_call | solution.py:423
  44.9 16.7 %collective-permute-done.2.refs_4_ = bf16[2,2048,128]{2,1,0:T(8,128)(2,1)S(1)} collective-permute-done((bf16[2,2048,128]{2,1,0:T(8,128)(2,1)}, bf16[2,2048,128]{2,1,0:T(8,128)(2,1)S(1)}, u32[]{:S(2)}, u32[]{:S(2)}) %collective-permute-start.2) | collective-permute-done | bytes 1048608 | tf_op jit(solution)/shard_map/ppermute | solution.py:40
  61.6 0.0 collective-permute-start.3
  61.6 0.0 collective-permute-done.4.refs_6_
  61.6 0.5 collective-permute-start.5
  62.1 0.0 collective-permute-done.6.refs_8_
  62.1 0.1 collective-permute-start.7
  62.2 0.0 collective-permute-done.8.refs_10_
  62.2 0.8 collective-permute-start.9
  63.0 2.2 %own.3.refs_12_ = f32[8,128,1152]{2,1,0:T(8,128)S(1)} custom-call(s32[8,128]{1,0:T(8,128)S(1)} %copy-done.1, bf16[512,2048]{1,0:T(8,128)(2,1)} %bitcast.3.queries, bf16[8192,256]{1,0:T(8,128)(2,1)} %refs_0_.5, bf16[8192,256]{1,0:T(8,128)(2,1)} %refs_1_.5, bf16[8192,256]{1,0:T(8,128)(2,1)} %collective-permute-done.near_keys.refs_2_, ...), custom_call_target="tpu_custom_call" | custom-call | flops 20000000000 | bytes 33554432 | tf_op jit(solution)/shard_map/own/pallas_call | solution.py:423
  65.2 0.0 collective-permute-done.3.refs_5_
  65.2 2.0 %collective-permute-done.5.refs_7_ = bf16[2,2048,128]{2,1,0:T(8,128)(2,1)S(1)} collective-permute-done((bf16[2,2048,128]{2,1,0:T(8,128)(2,1)S(1)}, bf16[2,2048,128]{2,1,0:T(8,128)(2,1)S(1)}, u32[]{:S(2)}, u32[]{:S(2)}) %collective-permute-start.5) | collective-permute-done | bytes 1048608 | tf_op jit(solution)/shard_map/ppermute | solution.py:30
  67.2 1.5 %collective-permute-done.7.refs_9_ = bf16[2,2048,128]{2,1,0:T(8,128)(2,1)S(1)} collective-permute-done((bf16[2,2048,128]{2,1,0:T(8,128)(2,1)S(1)}, bf16[2,2048,128]{2,1,0:T(8,128)(2,1)S(1)}, u32[]{:S(2)}, u32[]{:S(2)}) %collective-permute-start.7) | collective-permute-done | bytes 1048608 | tf_op jit(solution)/shard_map/ppermute | solution.py:30
  68.7 0.0 collective-permute-done.9.refs_11_
  68.8 26.4 %handed.1 = bf16[4,128,2176]{2,1,0:T(8,128)(2,1)S(1)} custom-call(s32[8,128]{1,0:T(8,128)S(1)} %copy-done.1, bf16[512,2048]{1,0:T(8,128)(2,1)} %bitcast.3.queries, bf16[8192,256]{1,0:T(8,128)(2,1)} %refs_0_.5, bf16[8192,256]{1,0:T(8,128)(2,1)} %refs_1_.5, bf16[8192,256]{1,0:T(8,128)(2,1)} %collective-permute-done.near_keys.refs_2_, ...), custom_call_target="tpu_custom_call" | custom-call | flops 20000000000 | bytes 33554432 | tf_op jit(solution)/shard_map/handed/pallas_call | solution.py:423
  95.1 47.5 %all_to_all.10.parts = bf16[16,32,2176]{2,1,0:T(8,128)(2,1)} all-to-all(bf16[16,32,2176]{2,1,0:T(8,128)(2,1)S(1)} %bitcast.6), channel_id=1, replica_groups=mesh['x'=4,'y'=4,'core'=2,'head'=4] {'x','y'}, dimensions={0} | all-to-all | bytes 4456448 | tf_op jit(solution)/shard_map/all_to_all | solution.py:460
  142.6 3.7 %finish.1 = bf16[32,2048]{1,0:T(8,128)(2,1)} custom-call(bf16[16,32,2176]{2,1,0:T(8,128)(2,1)} %all_to_all.10.parts), custom_call_target="tpu_custom_call" | custom-call | tf_op jit(solution)/shard_map/finish/pallas_call | solution.py:463
Async XLA Ops:
  0.0 16.6 %collective-permute-start = (bf16[8192,256]{1,0:T(8,128)(2,1)}, bf16[8192,256]{1,0:T(8,128)(2,1)}, u32[]{:S(2)}, u32[]{:S(2)}) collective-permute-start(bf16[8192,256]{1,0:T(8,128)(2,1)} %refs_0_.5), channel_id=1, source_target_pairs={{0,4},{4,0},{1,5},{5,1},{2,6},{6,2},{3,7},{7,3},{8,12},{12,8},{9,1... | collective-permute-start | bytes 12582920 | tf_op jit(solution)/shard_map/ppermute | solution.py:30
  0.0 16.6 %collective-permute-start.1 = (bf16[8192,256]{1,0:T(8,128)(2,1)}, bf16[8192,256]{1,0:T(8,128)(2,1)}, u32[]{:S(2)}, u32[]{:S(2)}) collective-permute-start(bf16[8192,256]{1,0:T(8,128)(2,1)} %refs_1_.5), channel_id=1, source_target_pairs={{0,4},{4,0},{1,5},{5,1},{2,6},{6,2},{3,7},{7,3},{8,12},{12,8},{9,1... | collective-permute-start | bytes 12582920 | tf_op jit(solution)/shard_map/ppermute | solution.py:30
  3.0 39.8 %all-to-all-start = ((bf16[64,8,2048]{2,1,0:T(8,128)(2,1)}), bf16[64,8,2048]{2,1,0:T(8,128)(2,1)}, u32[]{:S(2)}, u32[]{:S(2)}) async-start(bf16[64,8,2048]{2,1,0:T(8,128)(2,1)} %bitcast.2), calls=%async_computation | async-start | bytes 4194304 | tf_op jit(solution)/shard_map/all_to_all | solution.py:474
  16.6 0.7 copy-start
  17.3 25.5 %copy-start.1 = (s32[8,128]{1,0:T(8,128)S(1)}, s32[8,128]{1,0:T(8,128)}, u32[]{:S(2)}) copy-start(s32[8,128]{1,0:T(8,128)} %plan.1.table) | copy-start | bytes 12292
  22.9 38.7 %collective-permute-start.2 = (bf16[2,2048,128]{2,1,0:T(8,128)(2,1)}, bf16[2,2048,128]{2,1,0:T(8,128)(2,1)S(1)}, u32[]{:S(2)}, u32[]{:S(2)}) collective-permute-start(bf16[2,2048,128]{2,1,0:T(8,128)(2,1)} %get-tuple-element.9), channel_id=1, source_target_pairs={{0,32},{32,64},{64,96},{96,0},{1,33},{33,65},{65,97},{97,1},{2,34}... | collective-permute-start | bytes 3145736 | tf_op jit(solution)/shard_map/ppermute | solution.py:40
  23.6 37.9 %collective-permute-start.4 = (bf16[2,2048,128]{2,1,0:T(8,128)(2,1)}, bf16[2,2048,128]{2,1,0:T(8,128)(2,1)S(1)}, u32[]{:S(2)}, u32[]{:S(2)}) collective-permute-start(bf16[2,2048,128]{2,1,0:T(8,128)(2,1)} %get-tuple-element.10), channel_id=1, source_target_pairs={{0,96},{32,0},{64,32},{96,64},{1,97},{33,1},{65,33},{97,65},{2,98}... | collective-permute-start | bytes 3145736 | tf_op jit(solution)/shard_map/ppermute | solution.py:40
  26.2 35.9 %collective-permute-start.6 = (bf16[2,2048,128]{2,1,0:T(8,128)(2,1)}, bf16[2,2048,128]{2,1,0:T(8,128)(2,1)S(1)}, u32[]{:S(2)}, u32[]{:S(2)}) collective-permute-start(bf16[2,2048,128]{2,1,0:T(8,128)(2,1)} %get-tuple-element.11), channel_id=1, source_target_pairs={{0,8},{8,16},{16,24},{24,0},{1,9},{9,17},{17,25},{25,1},{2,10},{10... | collective-permute-start | bytes 3145736 | tf_op jit(solution)/shard_map/ppermute | solution.py:40
  27.0 35.2 %collective-permute-start.8 = (bf16[2,2048,128]{2,1,0:T(8,128)(2,1)}, bf16[2,2048,128]{2,1,0:T(8,128)(2,1)}, u32[]{:S(2)}, u32[]{:S(2)}) collective-permute-start(bf16[2,2048,128]{2,1,0:T(8,128)(2,1)} %get-tuple-element.12), channel_id=1, source_target_pairs={{0,24},{8,0},{16,8},{24,16},{1,25},{9,1},{17,9},{25,17},{2,26},{10... | collective-permute-start | bytes 3145736 | tf_op jit(solution)/shard_map/ppermute | solution.py:40
  61.6 3.6 %collective-permute-start.3 = (bf16[2,2048,128]{2,1,0:T(8,128)(2,1)S(1)}, bf16[2,2048,128]{2,1,0:T(8,128)(2,1)S(1)}, u32[]{:S(2)}, u32[]{:S(2)}) collective-permute-start(bf16[2,2048,128]{2,1,0:T(8,128)(2,1)S(1)} %collective-permute-done.2.refs_4_), channel_id=1, source_target_pairs={{0,4},{4,0},{1,5},{5,1},{2,6},{6,2},{3,7},{7,3},{8,12},{12,8},{9,1... | collective-permute-start | bytes 3145736 | tf_op jit(solution)/shard_map/ppermute | solution.py:30
  61.6 5.7 %collective-permute-start.5 = (bf16[2,2048,128]{2,1,0:T(8,128)(2,1)S(1)}, bf16[2,2048,128]{2,1,0:T(8,128)(2,1)S(1)}, u32[]{:S(2)}, u32[]{:S(2)}) collective-permute-start(bf16[2,2048,128]{2,1,0:T(8,128)(2,1)S(1)} %collective-permute-done.4.refs_6_), channel_id=1, source_target_pairs={{0,4},{4,0},{1,5},{5,1},{2,6},{6,2},{3,7},{7,3},{8,12},{12,8},{9,1... | collective-permute-start | bytes 3145736 | tf_op jit(solution)/shard_map/ppermute | solution.py:30
  62.1 6.6 %collective-permute-start.7 = (bf16[2,2048,128]{2,1,0:T(8,128)(2,1)S(1)}, bf16[2,2048,128]{2,1,0:T(8,128)(2,1)S(1)}, u32[]{:S(2)}, u32[]{:S(2)}) collective-permute-start(bf16[2,2048,128]{2,1,0:T(8,128)(2,1)S(1)} %collective-permute-done.6.refs_8_), channel_id=1, source_target_pairs={{0,4},{4,0},{1,5},{5,1},{2,6},{6,2},{3,7},{7,3},{8,12},{12,8},{9,1... | collective-permute-start | bytes 3145736 | tf_op jit(solution)/shard_map/ppermute | solution.py:30
  62.2 6.6 %collective-permute-start.9 = (bf16[2,2048,128]{2,1,0:T(8,128)(2,1)}, bf16[2,2048,128]{2,1,0:T(8,128)(2,1)S(1)}, u32[]{:S(2)}, u32[]{:S(2)}) collective-permute-start(bf16[2,2048,128]{2,1,0:T(8,128)(2,1)} %collective-permute-done.8.refs_10_), channel_id=1, source_target_pairs={{0,4},{4,0},{1,5},{5,1},{2,6},{6,2},{3,7},{7,3},{8,12},{12,8},{9,1... | collective-permute-start | bytes 3145736 | tf_op jit(solution)/shard_map/ppermute | solution.py:30

commit v3 on v2

--- a/solution.py
+++ b/solution.py
@@ -22,6 +22,8 @@
 ROOM = 36 * 2**20
 EARLY, LATER = 3, 5
 HALF = BLOCK // 2
+SPAN = 2048
+TILE = 512
 ARRIVAL = 5
 DIRECTIONS = ((1, 0), (-1, 0), (0, 1), (0, -1))
 
@@ -166,7 +168,7 @@
     )(table, *sources)
 
 
-def attention_kernel(table, queries, *refs, first, limit):
+def attention_kernel(table, left, right, *refs, first, limit):
     final = limit is None
     sources, refs = refs[: 12 if final else 4], refs[12 if final else 4 :]
     if first:
@@ -256,9 +258,16 @@
         return pl.ds(pl.multiple_of((task // 4) * WIDE + h * HEAD, HEAD), HEAD)
 
     def load(task):
-        tokens = pl.ds(pl.multiple_of((task % 4) * ROWS, ROWS), ROWS)
-        for h in range(GROUP):
-            stacked[h * ROWS : (h + 1) * ROWS, :] = queries[tokens, columns(task, h)]
+        q = task % 4
+        for head in range(2):
+
+            @pl.when(task // 4 == head)
+            def _():
+                for h in range(GROUP):
+                    for y in range(4):
+                        at = h * ROWS + y * CHUNK
+                        part = left[q, y] if head == 0 else right[y, q]
+                        stacked[at : at + CHUNK, :] = part[:, h * HEAD : (h + 1) * HEAD]
 
         @pl.when(touched[task] == 0)
         def _():
@@ -276,35 +285,33 @@
                     peak[rows, :] = jnp.broadcast_to(level, (ROWS, HEAD))
                     total[rows, :HEAD] = before[task, :, h * HEAD : (h + 1) * HEAD]
 
-    tile = 2 * ROWS
-
     def attend(task, slot, masked):
-        keys = key_buffer[slot]
-        values = jnp.concatenate(
-            [value_buffer[slot], jnp.ones((BLOCK, HEAD), jnp.bfloat16)], axis=1
-        )
-
-        def score(r):
+        steps = [(k, r) for k in range(0, BLOCK, SPAN) for r in range(0, GROUP * ROWS, TILE)]
+
+        def score(k, r):
+            keys = key_buffer[slot, k : k + SPAN, :]
             return lax.dot_general(
-                stacked[r : r + tile, :], keys, NT, preferred_element_type=jnp.float32
+                stacked[r : r + TILE, :], keys, NT, preferred_element_type=jnp.float32
             )
 
-        s = score(0)
-        for r in range(0, GROUP * ROWS, tile):
-            after = score(r + tile) if r + tile < GROUP * ROWS else None
-            if masked:
-                row = lax.broadcasted_iota(jnp.int32, (tile, 1024), 0) % ROWS
+        s = score(*steps[0])
+        for i, (k, r) in enumerate(steps):
+            after = score(*steps[i + 1]) if i + 1 < len(steps) else None
+            if masked and k + SPAN == BLOCK:
+                row = lax.broadcasted_iota(jnp.int32, (TILE, 1024), 0) % ROWS
                 token = (task % 4) * 256 + (row // CHUNK) * 64 + core * CHUNK + row % CHUNK
-                col = lax.broadcasted_iota(jnp.int32, (tile, 1024), 1)
-                s = jnp.concatenate(
-                    [s[:, :3072], jnp.where(col <= token, s[:, 3072:], NEG)], axis=1
-                )
-            rows = slice(r, r + tile)
+                col = lax.broadcasted_iota(jnp.int32, (TILE, 1024), 1)
+                tail = jnp.where(col <= token, s[:, SPAN - 1024 :], NEG)
+                s = jnp.concatenate([s[:, : SPAN - 1024], tail], axis=1)
+            rows = slice(r, r + TILE)
             old = peak[rows, :]
             new = jnp.maximum(old, jnp.max(s, axis=1, keepdims=True) * SCALE)
             factor = jnp.exp2(old - new)
             weights = jnp.exp2(s * SCALE - new[:, :1]).astype(jnp.bfloat16)
             peak[rows, :] = new
+            values = jnp.concatenate(
+                [value_buffer[slot, k : k + SPAN, :], jnp.ones((SPAN, HEAD), jnp.bfloat16)], axis=1
+            )
             total[rows, :] = total[rows, :] * jnp.concatenate([factor, factor], axis=1) + jnp.dot(
                 weights, values, preferred_element_type=jnp.float32
             )
@@ -422,7 +429,7 @@
         shape = jax.ShapeDtypeStruct((8, ROWS, PACK), jnp.float32)
     return pl.pallas_call(
         functools.partial(attention_kernel, first=first, limit=limit),
-        in_specs=[smem, vmem] + [hbm] * len(sources) + [vmem] * len(before),
+        in_specs=[smem, vmem, vmem] + [hbm] * len(sources) + [vmem] * len(before),
         out_specs=vmem,
         out_shape=shape,
         scratch_shapes=[
@@ -439,7 +446,7 @@
         compiler_params=pltpu.CompilerParams(vmem_limit_bytes=ROOM),
         cost_estimate=pl.CostEstimate(flops=2 * 10**10, bytes_accessed=2**25, transcendentals=0),
         name="handed" if limit is None else "own",
-    )(table, queries, *sources, *before)
+    )(table, *queries, *sources, *before)
 
 
 def finish_kernel(parts, out):
@@ -468,15 +475,17 @@
     )(parts)
 
 
-def gather(queries):
-    columns = queries.reshape(8, 4, 2 * WIDE).transpose(1, 0, 2)
-    sent = jnp.broadcast_to(columns[None], (16, 4, 8, 2 * WIDE)).reshape(64, 8, 2 * WIDE)
-    got = lax.all_to_all(sent, ("x", "y", "head"), split_axis=0, concat_axis=0, tiled=True)
-    return got.reshape(4 * ROWS, 2 * WIDE)
+def gather(queries, head, axes):
+    columns = queries.reshape(8, 4, 2, WIDE)[:, :, head].transpose(1, 0, 2)
+    sent = jnp.broadcast_to(columns[None], (4, 4, 8, WIDE)).reshape(16, 8, WIDE)
+    got = lax.all_to_all(sent, (axes[0], "head"), split_axis=0, concat_axis=0, tiled=True)
+    sent = jnp.broadcast_to(got.reshape(1, ROWS, WIDE), (4, ROWS, WIDE))
+    got = lax.all_to_all(sent, axes[1], split_axis=0, concat_axis=0, tiled=True)
+    return got.reshape(4, 4, CHUNK, WIDE)
 
 
 def shards(queries, keys, values, gates):
-    gathered = gather(queries)
+    gathered = [gather(queries, 0, "yx"), gather(queries, 1, "xy")]
     table = plan(gates)
     sources = [in_hbm(a) for a in (keys, values, other_core(keys), other_core(values))]
 

time: 148 us -> 167 us (1.13)
  blocking collectives: 47.5 us -> 93.6 us
  waiting for transfers between devices: 33.4 us -> 0.03 us
  Pallas kernels: 42.7 us -> 54.2 us
  starting transfers between devices: 19.4 us -> 12.9 us
    all_to_all x0 -> x3, blocking collectives: none -> 43.7 us  [the longest x2 27.7 us: gather(): lax.all_to_all(sent, (axes[0], 'head'), split_axis=0, concat_axis=0, tile...]
    ppermute x4, waiting for transfers between devices: 16.7 us -> 0.01 us  [hand_on(): return lax.ppermute(array, axis, [(i, (i + step) % 4) for i in range(4)])]
    all_to_all x1, waiting for transfers between devices: 13.2 us -> 0.01 us  [gather(): got = lax.all_to_all(sent, axes[1], split_axis=0, concat_axis=0, tiled=True)]
    pallas_call x3, Pallas kernels: 30.7 us -> 42.2 us  [attention(): pl.pallas_call(functools.partial(attention_kernel, first=first, limit=lim...]
    all_to_all x1, starting transfers between devices: 10.8 us -> 4.25 us  [gather(): got = lax.all_to_all(sent, axes[1], split_axis=0, concat_axis=0, tiled=True)]
    ppermute x6, waiting for transfers between devices: 3.53 us -> 0.02 us  [other_core(): return lax.ppermute(array, 'core', [(0, 1), (1, 0)])]
    all_to_all x1, blocking collectives: 47.5 us -> 49.9 us  [finish(): lax.all_to_all(partial.reshape(16, CHUNK, BOTH), ('x', 'y'), split_axis=0...]
  transfers between devices with their start and end apart: 11 -> 11, of which waited for: 4 -> 0; matrix products, arithmetic and copies ran while one was open for 2% -> 1% of each run, Pallas kernels for 9% -> 22%
where the time goes in v3:
time: 167 us; the launch traced here: 164 us
  blocking collectives  93.6 us (56%)
  Pallas kernels  54.2 us (32%)
  starting transfers between devices  12.9 us (8%)
  local copies, waits for them, and re-layouts  2.98 us (2%)
    all_to_all x1, blocking collectives, finish(): lax.all_to_all(partial.reshape(16, CHUNK, BOTH), ('x', 'y'), split_axis=0...  49.9 us
    pallas_call x3, Pallas kernels, attention(): pl.pallas_call(functools.partial(attention_kernel, first=first, limit=lim...  42.2 us
    all_to_all x2, blocking collectives, gather(): lax.all_to_all(sent, (axes[0], 'head'), split_axis=0, concat_axis=0, tile...  27.7 us
    all_to_all x1, blocking collectives, gather(): got = lax.all_to_all(sent, axes[1], split_axis=0, concat_axis=0, tiled=True)  16 us
    ppermute x4, starting transfers between devices, hand_on(): return lax.ppermute(array, axis, [(i, (i + step) % 4) for i in range(4)])  6.7 us
    pallas_call x1, Pallas kernels, ship(): pl.pallas_call(ship_kernel, in_specs=[pl.BlockSpec(memory_space=pltpu.SME...  5.61 us
    all_to_all x1, starting transfers between devices, gather(): got = lax.all_to_all(sent, axes[1], split_axis=0, concat_axis=0, tiled=True)  4.25 us
    pallas_call x1, Pallas kernels, finish(): pl.pallas_call(finish_kernel, out_shape=jax.ShapeDtypeStruct((CHUNK, 2 *...  3.65 us
  transfers between devices with their start and end apart: 11, of which 0 were waited for; matrix products, arithmetic and copies ran while one was open for 1% of the time, Pallas kernels for 22%

profile of v3, /device:TPU:64, one launch (start us, length us, event | category | flops | bytes accessed | tf_op | source)
XLA Modules:
  0.0 164.1 jit_solution(7950701429915889100)
XLA Ops:
  0.0 0.0 collective-permute-start
  0.0 0.5 collective-permute-start.1
  0.5 0.9 slice_bitcast_fusion
  1.4 13.9 %all_to_all.25 = bf16[16,8,1024]{2,1,0:T(8,128)(2,1)S(1)} all-to-all(bf16[16,8,1024]{2,1,0:T(8,128)(2,1)S(1)} %bitcast.22), channel_id=1, replica_groups=mesh['x'=4,'y'=4,'core'=2,'head'=4] {'x','head'}, dimensions={0} | all-to-all | bytes 524288 | tf_op jit(solution)/shard_map/all_to_all | solution.py:481
  15.4 13.8 %all_to_all.26 = bf16[16,8,1024]{2,1,0:T(8,128)(2,1)S(1)} all-to-all(bf16[16,8,1024]{2,1,0:T(8,128)(2,1)S(1)} %bitcast.23), channel_id=1, replica_groups=mesh['x'=4,'y'=4,'core'=2,'head'=4] {'y','head'}, dimensions={0} | all-to-all | bytes 524288 | tf_op jit(solution)/shard_map/all_to_all | solution.py:481
  29.2 0.1 broadcast_in_dim.31
  29.3 16.0 %all_to_all.27 = bf16[4,128,1024]{2,1,0:T(8,128)(2,1)} all-to-all(bf16[4,128,1024]{2,1,0:T(8,128)(2,1)S(1)} %broadcast_in_dim.31), channel_id=1, replica_groups=mesh['x'=4,'y'=4,'core'=2,'head'=4] {'y'}, dimensions={0} | all-to-all | bytes 2097152 | tf_op jit(solution)/shard_map/all_to_all | solution.py:483
  45.3 1.2 broadcast_in_dim.28
  46.4 4.3 %all-to-all-start.1 = ((bf16[4,128,1024]{2,1,0:T(8,128)(2,1)}), bf16[4,128,1024]{2,1,0:T(8,128)(2,1)}, u32[]{:S(2)}, u32[]{:S(2)}) async-start(bf16[4,128,1024]{2,1,0:T(8,128)(2,1)} %broadcast_in_dim.28), calls=%async_computation.1 | async-start | bytes 2097152 | tf_op jit(solution)/shard_map/all_to_all | solution.py:483
  50.7 2.8 %plan.1.table = s32[8,128]{1,0:T(8,128)} custom-call(s32[4,8,12]{2,1,0:T(8,128)} %gates.1), custom_call_target="tpu_custom_call" | custom-call | tf_op jit(solution)/shard_map/plan/pallas_call | solution.py:124
  53.5 0.0 copy-start
  53.5 0.0 collective-permute-done.near_keys.refs_2_
  53.5 0.0 collective-permute-done.1.near_values.refs_3_
  53.5 0.0 copy-start.1
  53.5 0.8 copy-done.1
  54.3 0.0 copy-start.2
  54.3 5.6 %ship.1 = (bf16[2,2048,128]{2,1,0:T(8,128)(2,1)}, bf16[2,2048,128]{2,1,0:T(8,128)(2,1)}, bf16[2,2048,128]{2,1,0:T(8,128)(2,1)}, bf16[2,2048,128]{2,1,0:T(8,128)(2,1)}) custom-call(s32[8,128]{1,0:T(8,128)S(1)} %copy-done.1, bf16[8192,256]{1,0:T(8,128)(2,1)} %refs_0_.5, bf16[8192,256]{1,0:T(8,128)(2,1)} %refs_1_.5, ...), custom_call_target="tpu_custom_call" | custom-call | bytes 1024 | tf_op jit(solution)/shard_map/ship/pallas_call | solution.py:159
  59.9 2.0 %collective-permute-start.2 = (bf16[2,2048,128]{2,1,0:T(8,128)(2,1)}, bf16[2,2048,128]{2,1,0:T(8,128)(2,1)S(1)}, u32[]{:S(2)}, u32[]{:S(2)}) collective-permute-start(bf16[2,2048,128]{2,1,0:T(8,128)(2,1)} %get-tuple-element.9), channel_id=1, source_target_pairs={{0,32},{32,64},{64,96},{96,0},{1,33},{33,65},{65,97},{97,1},{2,34}... | collective-permute-start | bytes 3145736 | tf_op jit(solution)/shard_map/ppermute | solution.py:42
  61.9 1.3 collective-permute-start.4
  63.2 0.6 collective-permute-start.6
  63.8 2.8 %collective-permute-start.8 = (bf16[2,2048,128]{2,1,0:T(8,128)(2,1)}, bf16[2,2048,128]{2,1,0:T(8,128)(2,1)}, u32[]{:S(2)}, u32[]{:S(2)}) collective-permute-start(bf16[2,2048,128]{2,1,0:T(8,128)(2,1)} %get-tuple-element.12), channel_id=1, source_target_pairs={{0,24},{8,0},{16,8},{24,16},{1,25},{9,1},{17,9},{25,17},{2,26},{10... | collective-permute-start | bytes 3145736 | tf_op jit(solution)/shard_map/ppermute | solution.py:42
  66.6 0.0 all-to-all-done.1
  66.6 0.0 copy-done
  66.6 0.0 copy-done.2
  66.6 19.1 %own.2.refs_4_ = f32[8,128,1152]{2,1,0:T(8,128)S(1)} custom-call(s32[8,128]{1,0:T(8,128)S(1)} %copy-done.2, bf16[4,4,32,1024]{3,2,1,0:T(8,128)(2,1)} %bitcast.5.left, bf16[4,4,32,1024]{3,2,1,0:T(8,128)(2,1)S(1)} %bitcast.17, bf16[8192,256]{1,0:T(8,128)(2,1)} %refs_0_.5, bf16[8192,256]{1,0:T(8,128)(2,1)} %refs_1_.5, ...), custom_call_target="tpu_custom_call" | custom-call | flops 20000000000 | bytes 33554432 | tf_op jit(solution)/shard_map/own/pallas_call | solution.py:430
  85.7 0.0 collective-permute-done.2.refs_4_
  85.7 0.1 collective-permute-start.3
  85.8 0.0 collective-permute-done.4.refs_6_
  85.8 0.5 collective-permute-start.5
  86.3 0.0 collective-permute-done.6.refs_8_
  86.3 0.1 collective-permute-start.7
  86.4 0.0 collective-permute-done.8.refs_10_
  86.4 0.8 collective-permute-start.9
  87.2 8.3 %own.3.refs_12_ = f32[8,128,1152]{2,1,0:T(8,128)S(1)} custom-call(s32[8,128]{1,0:T(8,128)S(1)} %copy-done.2, bf16[4,4,32,1024]{3,2,1,0:T(8,128)(2,1)} %bitcast.5.left, bf16[4,4,32,1024]{3,2,1,0:T(8,128)(2,1)S(1)} %bitcast.18, bf16[8192,256]{1,0:T(8,128)(2,1)} %refs_0_.5, bf16[8192,256]{1,0:T(8,128)(2,1)} %refs_1_.5, ...), custom_call_target="tpu_custom_call" | custom-call | flops 20000000000 | bytes 33554432 | tf_op jit(solution)/shard_map/own/pallas_call | solution.py:430
  95.5 0.0 collective-permute-done.3.refs_5_
  95.5 0.0 collective-permute-done.5.refs_7_
  95.5 0.0 collective-permute-done.7.refs_9_
  95.5 0.0 collective-permute-done.9.refs_11_
  95.5 14.8 %handed.1 = bf16[4,128,2176]{2,1,0:T(8,128)(2,1)S(1)} custom-call(s32[8,128]{1,0:T(8,128)S(1)} %copy-done.2, bf16[4,4,32,1024]{3,2,1,0:T(8,128)(2,1)} %bitcast.5.left, bf16[4,4,32,1024]{3,2,1,0:T(8,128)(2,1)S(1)} %bitcast.19, bf16[8192,256]{1,0:T(8,128)(2,1)} %refs_0_.5, bf16[8192,256]{1,0:T(8,128)(2,1)} %refs_1_.5, ...), custom_call_target="tpu_custom_call" | custom-call | flops 20000000000 | bytes 33554432 | tf_op jit(solution)/shard_map/handed/pallas_call | solution.py:430
  110.3 49.9 %all_to_all.28.parts = bf16[16,32,2176]{2,1,0:T(8,128)(2,1)} all-to-all(bf16[16,32,2176]{2,1,0:T(8,128)(2,1)S(1)} %bitcast.16), channel_id=1, replica_groups=mesh['x'=4,'y'=4,'core'=2,'head'=4] {'x','y'}, dimensions={0} | all-to-all | bytes 4456448 | tf_op jit(solution)/shard_map/all_to_all | solution.py:467
  160.3 3.7 %finish.1 = bf16[32,2048]{1,0:T(8,128)(2,1)} custom-call(bf16[16,32,2176]{2,1,0:T(8,128)(2,1)} %all_to_all.28.parts), custom_call_target="tpu_custom_call" | custom-call | tf_op jit(solution)/shard_map/finish/pallas_call | solution.py:470
  (2 shorter events, 0.0 us)
Async XLA Ops:
  0.0 53.5 %collective-permute-start = (bf16[8192,256]{1,0:T(8,128)(2,1)}, bf16[8192,256]{1,0:T(8,128)(2,1)}, u32[]{:S(2)}, u32[]{:S(2)}) collective-permute-start(bf16[8192,256]{1,0:T(8,128)(2,1)} %refs_0_.5), channel_id=1, source_target_pairs={{0,4},{4,0},{1,5},{5,1},{2,6},{6,2},{3,7},{7,3},{8,12},{12,8},{9,1... | collective-permute-start | bytes 12582920 | tf_op jit(solution)/shard_map/ppermute | solution.py:32
  0.0 53.5 %collective-permute-start.1 = (bf16[8192,256]{1,0:T(8,128)(2,1)}, bf16[8192,256]{1,0:T(8,128)(2,1)}, u32[]{:S(2)}, u32[]{:S(2)}) collective-permute-start(bf16[8192,256]{1,0:T(8,128)(2,1)} %refs_1_.5), channel_id=1, source_target_pairs={{0,4},{4,0},{1,5},{5,1},{2,6},{6,2},{3,7},{7,3},{8,12},{12,8},{9,1... | collective-permute-start | bytes 12582920 | tf_op jit(solution)/shard_map/ppermute | solution.py:32
  46.4 20.2 %all-to-all-start.1 = ((bf16[4,128,1024]{2,1,0:T(8,128)(2,1)}), bf16[4,128,1024]{2,1,0:T(8,128)(2,1)}, u32[]{:S(2)}, u32[]{:S(2)}) async-start(bf16[4,128,1024]{2,1,0:T(8,128)(2,1)} %broadcast_in_dim.28), calls=%async_computation.1 | async-start | bytes 2097152 | tf_op jit(solution)/shard_map/all_to_all | solution.py:483
  53.5 13.1 %copy-start = (bf16[4,128,1024]{2,1,0:T(8,128)(2,1)S(1)}, bf16[4,128,1024]{2,1,0:T(8,128)(2,1)}, u32[]{:S(2)}) copy-start(bf16[4,128,1024]{2,1,0:T(8,128)(2,1)} %all_to_all.27) | copy-start | bytes 3145732
  53.5 0.8 copy-start.1
  54.3 12.3 %copy-start.2 = (s32[8,128]{1,0:T(8,128)S(1)}, s32[8,128]{1,0:T(8,128)}, u32[]{:S(2)}) copy-start(s32[8,128]{1,0:T(8,128)} %plan.1.table) | copy-start | bytes 12292
  59.9 25.8 %collective-permute-start.2 = (bf16[2,2048,128]{2,1,0:T(8,128)(2,1)}, bf16[2,2048,128]{2,1,0:T(8,128)(2,1)S(1)}, u32[]{:S(2)}, u32[]{:S(2)}) collective-permute-start(bf16[2,2048,128]{2,1,0:T(8,128)(2,1)} %get-tuple-element.9), channel_id=1, source_target_pairs={{0,32},{32,64},{64,96},{96,0},{1,33},{33,65},{65,97},{97,1},{2,34}... | collective-permute-start | bytes 3145736 | tf_op jit(solution)/shard_map/ppermute | solution.py:42
  61.9 23.8 %collective-permute-start.4 = (bf16[2,2048,128]{2,1,0:T(8,128)(2,1)}, bf16[2,2048,128]{2,1,0:T(8,128)(2,1)S(1)}, u32[]{:S(2)}, u32[]{:S(2)}) collective-permute-start(bf16[2,2048,128]{2,1,0:T(8,128)(2,1)} %get-tuple-element.10), channel_id=1, source_target_pairs={{0,96},{32,0},{64,32},{96,64},{1,97},{33,1},{65,33},{97,65},{2,98}... | collective-permute-start | bytes 3145736 | tf_op jit(solution)/shard_map/ppermute | solution.py:42
  63.2 23.1 %collective-permute-start.6 = (bf16[2,2048,128]{2,1,0:T(8,128)(2,1)}, bf16[2,2048,128]{2,1,0:T(8,128)(2,1)}, u32[]{:S(2)}, u32[]{:S(2)}) collective-permute-start(bf16[2,2048,128]{2,1,0:T(8,128)(2,1)} %get-tuple-element.11), channel_id=1, source_target_pairs={{0,8},{8,16},{16,24},{24,0},{1,9},{9,17},{17,25},{25,1},{2,10},{10... | collective-permute-start | bytes 3145736 | tf_op jit(solution)/shard_map/ppermute | solution.py:42
  63.8 22.6 %collective-permute-start.8 = (bf16[2,2048,128]{2,1,0:T(8,128)(2,1)}, bf16[2,2048,128]{2,1,0:T(8,128)(2,1)}, u32[]{:S(2)}, u32[]{:S(2)}) collective-permute-start(bf16[2,2048,128]{2,1,0:T(8,128)(2,1)} %get-tuple-element.12), channel_id=1, source_target_pairs={{0,24},{8,0},{16,8},{24,16},{1,25},{9,1},{17,9},{25,17},{2,26},{10... | collective-permute-start | bytes 3145736 | tf_op jit(solution)/shard_map/ppermute | solution.py:42
  85.7 9.8 %collective-permute-start.3 = (bf16[2,2048,128]{2,1,0:T(8,128)(2,1)S(1)}, bf16[2,2048,128]{2,1,0:T(8,128)(2,1)S(1)}, u32[]{:S(2)}, u32[]{:S(2)}) collective-permute-start(bf16[2,2048,128]{2,1,0:T(8,128)(2,1)S(1)} %collective-permute-done.2.refs_4_), channel_id=1, source_target_pairs={{0,4},{4,0},{1,5},{5,1},{2,6},{6,2},{3,7},{7,3},{8,12},{12,8},{9,1... | collective-permute-start | bytes 3145736 | tf_op jit(solution)/shard_map/ppermute | solution.py:32
  85.8 9.7 %collective-permute-start.5 = (bf16[2,2048,128]{2,1,0:T(8,128)(2,1)S(1)}, bf16[2,2048,128]{2,1,0:T(8,128)(2,1)S(1)}, u32[]{:S(2)}, u32[]{:S(2)}) collective-permute-start(bf16[2,2048,128]{2,1,0:T(8,128)(2,1)S(1)} %collective-permute-done.4.refs_6_), channel_id=1, source_target_pairs={{0,4},{4,0},{1,5},{5,1},{2,6},{6,2},{3,7},{7,3},{8,12},{12,8},{9,1... | collective-permute-start | bytes 3145736 | tf_op jit(solution)/shard_map/ppermute | solution.py:32
  86.3 9.2 %collective-permute-start.7 = (bf16[2,2048,128]{2,1,0:T(8,128)(2,1)}, bf16[2,2048,128]{2,1,0:T(8,128)(2,1)S(1)}, u32[]{:S(2)}, u32[]{:S(2)}) collective-permute-start(bf16[2,2048,128]{2,1,0:T(8,128)(2,1)} %collective-permute-done.6.refs_8_), channel_id=1, source_target_pairs={{0,4},{4,0},{1,5},{5,1},{2,6},{6,2},{3,7},{7,3},{8,12},{12,8},{9,1... | collective-permute-start | bytes 3145736 | tf_op jit(solution)/shard_map/ppermute | solution.py:32
  86.4 9.2 %collective-permute-start.9 = (bf16[2,2048,128]{2,1,0:T(8,128)(2,1)}, bf16[2,2048,128]{2,1,0:T(8,128)(2,1)S(1)}, u32[]{:S(2)}, u32[]{:S(2)}) collective-permute-start(bf16[2,2048,128]{2,1,0:T(8,128)(2,1)} %collective-permute-done.8.refs_10_), channel_id=1, source_target_pairs={{0,4},{4,0},{1,5},{5,1},{2,6},{6,2},{3,7},{7,3},{8,12},{12,8},{9,1... | collective-permute-start | bytes 3145736 | tf_op jit(solution)/shard_map/ppermute | solution.py:32
